TPU v7x, 128 devices: a whole 4x4x4 slice. The times are simulated.
128 devices in a mesh: section: 2 (over core), dp: 64 (over y, x, z).
Axes of the slice: x: 4, y: 4, z: 4, core: 2. Of those that a mesh axis runs over, the one named last changes fastest.
Arguments:
- window_input: bfloat16 [2, 64, 64, 1536], P(None, 'dp'), may hold values from -6 to 6
- cotangent: bfloat16 [2, 64, 64, 1536], P(None, 'dp'), may hold values from -6 to 6
- lengths: int32 [2, 64], P(None, 'dp'), may hold values from 1 to 64, as said below
- widths: int32 [2], replicated, may hold values from 768 to 6144, as said below
- gain_first: bfloat16 [2, 1536], P('section', 'dp'), may hold values from 0.5 to 1.5
- shift_first: bfloat16 [2, 1536], P('section', 'dp'), may hold values from -4 to 4
- project_weight: bfloat16 [2, 1536, 4608], P('section', 'dp'), may hold values from -0.15625 to 0.15625
- project_bias: bfloat16 [2, 4608], P('section', 'dp'), may hold values from -6 to 6
- output_weight: bfloat16 [2, 1536, 1536], P('section', 'dp'), may hold values from -0.625 to 0.625
- output_bias: bfloat16 [2, 1536], P('section', 'dp'), may hold values from -6 to 6
- gain_second: bfloat16 [2, 1536], P('section', 'dp'), may hold values from 0.5 to 1.5
- shift_second: bfloat16 [2, 1536], P('section', 'dp'), may hold values from -4 to 4
- expand_weight: bfloat16 [2, 1536, 6144], P('section', 'dp'), may hold values from -0.15625 to 0.15625
- expand_bias: bfloat16 [2, 6144], P('section', 'dp'), may hold values from -6 to 6
- shrink_weight: bfloat16 [2, 6144, 1536], P('section', 'dp'), may hold values from -0.15625 to 0.15625
- shrink_bias: bfloat16 [2, 1536], P('section', 'dp'), may hold values from -4 to 4
Outputs:
- activations: bfloat16 [2, 2, 64, 64, 1536], P('section', None, 'dp')
- input_grads: bfloat16 [2, 2, 64, 64, 1536], P('section', None, 'dp')
- grad_gain_first: float32 [2, 1536], P('section', 'dp')
- grad_shift_first: float32 [2, 1536], P('section', 'dp')
- grad_project_weight: float32 [2, 1536, 4608], P('section', 'dp')
- grad_project_bias: float32 [2, 4608], P('section', 'dp')
- grad_output_weight: float32 [2, 1536, 1536], P('section', 'dp')
- grad_output_bias: float32 [2, 1536], P('section', 'dp')
- grad_gain_second: float32 [2, 1536], P('section', 'dp')
- grad_shift_second: float32 [2, 1536], P('section', 'dp')
- grad_expand_weight: float32 [2, 1536, 6144], P('section', 'dp')
- grad_expand_bias: float32 [2, 6144], P('section', 'dp')
- grad_shrink_weight: float32 [2, 6144, 1536], P('section', 'dp')
- grad_shrink_bias: float32 [2, 1536], P('section', 'dp')
Inputs may be any that keep to these rules, and one draw needn't show every extreme that they name: `lengths`: in each micro-batch some sequence has all 64 tokens. `widths`: each is 6144, 3072, 1536 or 768; some micro-batch has 6144.
All inputs are finite; a program needn't handle non-finite values.
Results may differ from a plain program's by a relative error of at most 0.018.
Values may be sent and summed in bfloat16 or wider, within the bound.
A program may use at most 384 MiB of HBM per device.

v0:
```python
import jax
import jax.numpy as jnp
from jax import lax
from jax.sharding import PartitionSpec as P

HEADS = 12


EPS = 1e-05
MASKED = -1000000000.0


def from_behind(value, axis, by):
    count = lax.axis_size(axis)
    pairs = [(i, i + by) for i in range(count) if 0 <= i + by < count]
    return lax.ppermute(value, axis, pairs)


def norm_rows(values, norm_gain, norm_shift):
    row_mean = jnp.mean(values, axis=-1, keepdims=True)
    centred = values - row_mean
    row_var = jnp.mean(centred * centred, axis=-1, keepdims=True)
    return centred * lax.rsqrt(row_var + EPS) * norm_gain + norm_shift


def rotary_tables(seq_count, head_width):
    half_width = head_width // 2
    inverse_rates = 10000.0 ** (-jnp.arange(half_width, dtype=jnp.float32) / half_width)
    angles = jnp.arange(seq_count, dtype=jnp.float32)[:, None] * inverse_rates[None, :]
    return (jnp.cos(angles)[:, None, :], jnp.sin(angles)[:, None, :])


def rotate(vectors, cosine_table, sine_table):
    half_width = vectors.shape[-1] // 2
    front_half = vectors[..., :half_width]
    back_half = vectors[..., half_width:]
    return jnp.concatenate(
        [
            front_half * cosine_table - back_half * sine_table,
            back_half * cosine_table + front_half * sine_table,
        ],
        axis=-1,
    )


def unrotate(vectors, cosine_table, sine_table):
    half_width = vectors.shape[-1] // 2
    front_half = vectors[..., :half_width]
    back_half = vectors[..., half_width:]
    return jnp.concatenate(
        [
            front_half * cosine_table + back_half * sine_table,
            back_half * cosine_table - front_half * sine_table,
        ],
        axis=-1,
    )


def select_entry(table, position):
    clipped = jnp.clip(position, 0, table.shape[0] - 1)
    return jnp.sum(jnp.where(jnp.arange(table.shape[0]) == clipped, table, 0))


def live_mask(seq_count, seq_length):
    return (jnp.arange(seq_count) < seq_length).astype(jnp.float32)[:, None]


def width_level(prefix_width, full_width):
    return (
        (prefix_width < full_width).astype(jnp.int32)
        + (prefix_width < full_width // 2).astype(jnp.int32)
        + (prefix_width < full_width // 4).astype(jnp.int32)
    )


def attention_scores(queries, keys_turned, seq_length):
    seq_count = queries.shape[0]
    scores = jnp.einsum(
        "qhd,khd->hqk", queries, keys_turned, preferred_element_type=jnp.float32
    ) * queries.shape[-1] ** (-0.5)
    positions = jnp.arange(seq_count)
    visible = (positions[None, :] <= positions[:, None]) & (positions[None, :] < seq_length)
    return jnp.where(visible[None], scores, MASKED)


def second_normed(weights, middle):
    return norm_rows(middle, weights[6].astype(jnp.float32), weights[7].astype(jnp.float32)).astype(
        jnp.bfloat16
    )


def ffn_forward(weights, middle, prefix_width):
    normed_second = second_normed(weights, middle)
    full_width = weights[8].shape[1]

    def build_branch(width):

        def branch_run(normed_rows):
            upper_units = jnp.dot(
                normed_rows, weights[8][:, :width], preferred_element_type=jnp.float32
            ) + weights[9][:width].astype(jnp.float32)
            active = jax.nn.gelu(upper_units, approximate=True).astype(jnp.bfloat16)
            return jnp.dot(active, weights[10][:width], preferred_element_type=jnp.float32)

        return branch_run

    branches = [build_branch(full_width // 2**power) for power in range(4)]
    return lax.switch(width_level(prefix_width, full_width), branches, normed_second)


def layer_forward(weights, layer_in, seq_length, prefix_width):
    seq_count, model_width = layer_in.shape
    hidden = layer_in.astype(jnp.float32)
    normed = norm_rows(
        hidden, weights[0].astype(jnp.float32), weights[1].astype(jnp.float32)
    ).astype(jnp.bfloat16)
    joined = jnp.dot(normed, weights[2], preferred_element_type=jnp.float32) + weights[3].astype(
        jnp.float32
    )
    joined = joined.reshape(seq_count, 3, HEADS, model_width // HEADS)
    cosine_table, sine_table = rotary_tables(seq_count, model_width // HEADS)
    queries = rotate(joined[:, 0], cosine_table, sine_table).astype(jnp.bfloat16)
    keys_turned = rotate(joined[:, 1], cosine_table, sine_table).astype(jnp.bfloat16)
    values = joined[:, 2].astype(jnp.bfloat16)
    scores = attention_scores(queries, keys_turned, seq_length)
    row_top = jnp.max(scores, axis=-1, keepdims=True)
    log_total = row_top + jnp.log(jnp.sum(jnp.exp(scores - row_top), axis=-1, keepdims=True))
    attention = jnp.exp(scores - log_total).astype(jnp.bfloat16)
    mixed_heads = jnp.einsum("hqk,khd->qhd", attention, values, preferred_element_type=jnp.float32)
    mixed_heads = mixed_heads.reshape(seq_count, model_width).astype(jnp.bfloat16)
    middle = (
        hidden
        + jnp.dot(mixed_heads, weights[4], preferred_element_type=jnp.float32)
        + weights[5].astype(jnp.float32)
    )
    result = middle + ffn_forward(weights, middle, prefix_width) + weights[11].astype(jnp.float32)
    kept_state = (layer_in, normed, queries, keys_turned, values, log_total, mixed_heads, middle)
    return (result * live_mask(seq_count, seq_length), kept_state)


def ffn_backward(weights, middle, grad_rows, prefix_width):
    grad_low = grad_rows.astype(jnp.bfloat16)
    normed_second = second_normed(weights, middle)
    full_width = weights[8].shape[1]

    def build_branch(width):

        def branch_run(normed_rows, grad_part):
            upper_units = jnp.dot(
                normed_rows, weights[8][:, :width], preferred_element_type=jnp.float32
            ) + weights[9][:width].astype(jnp.float32)
            active_float, gelu_back = jax.vjp(
                lambda units: jax.nn.gelu(units, approximate=True), upper_units
            )
            active = active_float.astype(jnp.bfloat16)
            grad_active = jnp.einsum(
                "td,fd->tf", grad_part, weights[10][:width], preferred_element_type=jnp.float32
            )
            grad_upper = gelu_back(grad_active)[0].astype(jnp.bfloat16)
            grad_normed = jnp.einsum(
                "tf,df->td", grad_upper, weights[8][:, :width], preferred_element_type=jnp.float32
            )
            spare_rows = full_width - width
            return (
                grad_normed,
                jnp.pad(active, ((0, 0), (0, spare_rows))),
                jnp.pad(grad_upper, ((0, 0), (0, spare_rows))),
            )

        return branch_run

    branches = [build_branch(full_width // 2**power) for power in range(4)]
    grad_normed_second, active_rows, grad_upper_rows = lax.switch(
        width_level(prefix_width, full_width), branches, normed_second, grad_low
    )
    grad_shrink_bias = jnp.sum(grad_rows, axis=0)
    unused, norm_back_second = jax.vjp(
        norm_rows, middle, weights[6].astype(jnp.float32), weights[7].astype(jnp.float32)
    )
    middle_part, grad_gain_second, grad_shift_second = norm_back_second(grad_normed_second)
    grad_middle = grad_rows + middle_part
    small_terms = (grad_gain_second, grad_shift_second, grad_shrink_bias)
    row_parts = (normed_second, active_rows, grad_upper_rows, grad_low)
    return (grad_middle, small_terms, row_parts)


def attention_backward(weights, kept_state, grad_middle, seq_length):
    layer_in, normed, queries, keys_turned, values, log_total, mixed_heads, middle = kept_state
    seq_count, model_width = layer_in.shape
    hidden = layer_in.astype(jnp.float32)
    grad_branch = grad_middle.astype(jnp.bfloat16)
    grad_output_bias = jnp.sum(grad_branch.astype(jnp.float32), axis=0)
    grad_mixed = jnp.einsum(
        "te,de->td", grad_branch, weights[4], preferred_element_type=jnp.float32
    )
    grad_mixed = grad_mixed.astype(jnp.bfloat16).reshape(seq_count, HEADS, model_width // HEADS)
    scores = attention_scores(queries, keys_turned, seq_length)
    attention = jnp.exp(scores - log_total)
    attention_low = attention.astype(jnp.bfloat16)
    grad_values = jnp.einsum(
        "hqk,qhd->khd", attention_low, grad_mixed, preferred_element_type=jnp.float32
    )
    grad_attention = jnp.einsum(
        "qhd,khd->hqk", grad_mixed, values, preferred_element_type=jnp.float32
    )
    row_delta = jnp.sum(grad_attention * attention, axis=-1, keepdims=True)
    grad_scores = (attention * (grad_attention - row_delta)).astype(jnp.bfloat16)
    score_scale = queries.shape[-1] ** (-0.5)
    grad_queries = (
        jnp.einsum("hqk,khd->qhd", grad_scores, keys_turned, preferred_element_type=jnp.float32)
        * score_scale
    )
    grad_keys = (
        jnp.einsum("hqk,qhd->khd", grad_scores, queries, preferred_element_type=jnp.float32)
        * score_scale
    )
    cosine_table, sine_table = rotary_tables(seq_count, model_width // HEADS)
    grad_joined = jnp.stack(
        [
            unrotate(grad_queries, cosine_table, sine_table),
            unrotate(grad_keys, cosine_table, sine_table),
            grad_values,
        ],
        axis=1,
    )
    grad_joined = grad_joined.reshape(seq_count, 3 * model_width).astype(jnp.bfloat16)
    grad_project_bias = jnp.sum(grad_joined.astype(jnp.float32), axis=0)
    grad_normed = jnp.einsum(
        "te,de->td", grad_joined, weights[2], preferred_element_type=jnp.float32
    )
    unused, norm_back_first = jax.vjp(
        norm_rows, hidden, weights[0].astype(jnp.float32), weights[1].astype(jnp.float32)
    )
    hidden_part, grad_gain_first, grad_shift_first = norm_back_first(grad_normed)
    grad_hidden = grad_middle + hidden_part
    small_terms = (grad_gain_first, grad_shift_first, grad_project_bias, grad_output_bias)
    row_parts = (normed, grad_joined, mixed_heads, grad_branch)
    return (grad_hidden, small_terms, row_parts)


def accumulate(totals, terms):
    if totals is None:
        return tuple(terms)
    return tuple((running + fresh for running, fresh in zip(totals, terms)))


def join_rows(row_list):
    return tuple(
        (
            jnp.concatenate([parts[member] for parts in row_list], axis=0)
            for member in range(len(row_list[0]))
        )
    )


def ffn_totals_from(small_totals, row_list):
    normed_all, active_all, grad_upper_all, grad_all = join_rows(row_list)
    grad_expand = jnp.einsum(
        "td,tf->df", normed_all, grad_upper_all, preferred_element_type=jnp.float32
    )
    grad_expand_bias = jnp.sum(grad_upper_all.astype(jnp.float32), axis=0)
    grad_shrink = jnp.einsum("tf,td->fd", active_all, grad_all, preferred_element_type=jnp.float32)
    return (
        small_totals[0][None],
        small_totals[1][None],
        grad_expand[None],
        grad_expand_bias[None],
        grad_shrink[None],
        small_totals[2][None],
    )


def attention_totals_from(small_totals, row_list):
    normed_all, grad_joined_all, mixed_all, grad_branch_all = join_rows(row_list)
    grad_project = jnp.einsum(
        "td,te->de", normed_all, grad_joined_all, preferred_element_type=jnp.float32
    )
    grad_output = jnp.einsum(
        "td,te->de", mixed_all, grad_branch_all, preferred_element_type=jnp.float32
    )
    return (
        small_totals[0][None],
        small_totals[1][None],
        grad_project[None],
        small_totals[2][None],
        grad_output[None],
        small_totals[3][None],
    )


def per_device(
    window_input,
    cotangent,
    lengths,
    widths,
    gain_first,
    shift_first,
    project_weight,
    project_bias,
    output_weight,
    output_bias,
    gain_second,
    shift_second,
    expand_weight,
    expand_bias,
    shrink_weight,
    shrink_bias,
):
    section_index = lax.axis_index("section")
    is_first = section_index == 0
    gathered = (
        lax.all_gather(gain_first, "dp", axis=1, tiled=True),
        lax.all_gather(shift_first, "dp", axis=1, tiled=True),
        lax.all_gather(project_weight, "dp", axis=1, tiled=True),
        lax.all_gather(project_bias, "dp", axis=1, tiled=True),
        lax.all_gather(output_weight, "dp", axis=1, tiled=True),
        lax.all_gather(output_bias, "dp", axis=1, tiled=True),
        lax.all_gather(gain_second, "dp", axis=1, tiled=True),
        lax.all_gather(shift_second, "dp", axis=1, tiled=True),
        lax.all_gather(expand_weight, "dp", axis=1, tiled=True),
        lax.all_gather(expand_bias, "dp", axis=1, tiled=True),
        lax.all_gather(shrink_weight, "dp", axis=1, tiled=True),
        lax.all_gather(shrink_bias, "dp", axis=1, tiled=True),
    )
    weights = tuple((piece[0] for piece in gathered))
    micro_count = window_input.shape[0]
    seq_count = window_input.shape[2]
    model_width = window_input.shape[3]
    length_table = lengths[:, 0]
    empty_rows = jnp.zeros((seq_count, model_width), jnp.bfloat16)
    arriving = empty_rows
    produced = []
    kept_all = []
    for period in range(micro_count + 1):
        micro_index = period - section_index
        seq_length = select_entry(length_table, micro_index)
        prefix_width = select_entry(widths, micro_index)
        source = window_input[min(period, micro_count - 1), 0]
        layer_in = jnp.where(is_first, source, arriving)
        result, kept_state = layer_forward(weights, layer_in, seq_length, prefix_width)
        result = result.astype(jnp.bfloat16)
        produced.append(result)
        kept_all.append(kept_state)
        if period < micro_count:
            arriving = from_behind(result, "section", 1)
    activations = jnp.stack(
        [
            jnp.where(is_first, produced[micro_at], produced[micro_at + 1])
            for micro_at in range(micro_count)
        ]
    )
    activations = activations.reshape(1, micro_count, 1, seq_count, model_width)
    regathered = (
        lax.all_gather(gain_first, "dp", axis=1, tiled=True),
        lax.all_gather(shift_first, "dp", axis=1, tiled=True),
        lax.all_gather(project_weight, "dp", axis=1, tiled=True),
        lax.all_gather(project_bias, "dp", axis=1, tiled=True),
        lax.all_gather(output_weight, "dp", axis=1, tiled=True),
        lax.all_gather(output_bias, "dp", axis=1, tiled=True),
        lax.all_gather(gain_second, "dp", axis=1, tiled=True),
        lax.all_gather(shift_second, "dp", axis=1, tiled=True),
        lax.all_gather(expand_weight, "dp", axis=1, tiled=True),
        lax.all_gather(expand_bias, "dp", axis=1, tiled=True),
        lax.all_gather(shrink_weight, "dp", axis=1, tiled=True),
        lax.all_gather(shrink_bias, "dp", axis=1, tiled=True),
    )
    weights_back = tuple((piece[0] for piece in regathered))
    returning = empty_rows
    returned = []
    attention_small = None
    ffn_small = None
    attention_rows = []
    ffn_rows = []
    for period in range(micro_count + 1):
        micro_index = period - 1 + section_index
        seq_length = select_entry(length_table, micro_index)
        prefix_width = select_entry(widths, micro_index)
        incoming = cotangent[period, 0] if period < micro_count else empty_rows
        grad_in = jnp.where(is_first, returning, incoming)
        kept_state = jax.tree.map(
            lambda late_part, early_part: jnp.where(is_first, early_part, late_part),
            kept_all[min(period + 1, micro_count)],
            kept_all[max(period - 1, 0)],
        )
        grad_rows = grad_in.astype(jnp.float32) * live_mask(seq_count, seq_length)
        grad_middle, ffn_terms, ffn_parts = ffn_backward(
            weights_back, kept_state[7], grad_rows, prefix_width
        )
        ffn_small = accumulate(ffn_small, ffn_terms)
        ffn_rows.append(ffn_parts)
        grad_hidden, attention_terms, attention_parts = attention_backward(
            weights_back, kept_state, grad_middle, seq_length
        )
        attention_small = accumulate(attention_small, attention_terms)
        attention_rows.append(attention_parts)
        grad_low = grad_hidden.astype(jnp.bfloat16)
        returned.append(grad_low)
        if period < micro_count:
            returning = from_behind(grad_low, "section", -1)
    attention_totals = attention_totals_from(attention_small, attention_rows)
    ffn_totals = ffn_totals_from(ffn_small, ffn_rows)
    shares = (
        lax.psum_scatter(attention_totals[0], "dp", scatter_dimension=1, tiled=True),
        lax.psum_scatter(attention_totals[1], "dp", scatter_dimension=1, tiled=True),
        lax.psum_scatter(attention_totals[2], "dp", scatter_dimension=1, tiled=True),
        lax.psum_scatter(attention_totals[3], "dp", scatter_dimension=1, tiled=True),
        lax.psum_scatter(attention_totals[4], "dp", scatter_dimension=1, tiled=True),
        lax.psum_scatter(attention_totals[5], "dp", scatter_dimension=1, tiled=True),
        lax.psum_scatter(ffn_totals[0], "dp", scatter_dimension=1, tiled=True),
        lax.psum_scatter(ffn_totals[1], "dp", scatter_dimension=1, tiled=True),
        lax.psum_scatter(ffn_totals[2], "dp", scatter_dimension=1, tiled=True),
        lax.psum_scatter(ffn_totals[3], "dp", scatter_dimension=1, tiled=True),
        lax.psum_scatter(ffn_totals[4], "dp", scatter_dimension=1, tiled=True),
        lax.psum_scatter(ffn_totals[5], "dp", scatter_dimension=1, tiled=True),
    )
    input_grads = jnp.stack(
        [
            jnp.where(is_first, returned[micro_at + 1], returned[micro_at])
            for micro_at in range(micro_count)
        ]
    )
    input_grads = input_grads.reshape(1, micro_count, 1, seq_count, model_width)
    return (
        activations,
        input_grads,
        shares[0],
        shares[1],
        shares[2],
        shares[3],
        shares[4],
        shares[5],
        shares[6],
        shares[7],
        shares[8],
        shares[9],
        shares[10],
        shares[11],
    )


def solution(mesh):
    return jax.shard_map(
        per_device,
        mesh=mesh,
        in_specs=(
            P(None, "dp", None, None),
            P(None, "dp", None, None),
            P(None, "dp"),
            P(),
            P("section", "dp"),
            P("section", "dp"),
            P("section", "dp", None),
            P("section", "dp"),
            P("section", "dp", None),
            P("section", "dp"),
            P("section", "dp"),
            P("section", "dp"),
            P("section", "dp", None),
            P("section", "dp"),
            P("section", "dp", None),
            P("section", "dp"),
        ),
        out_specs=(
            P("section", None, "dp", None, None),
            P("section", None, "dp", None, None),
            P("section", "dp"),
            P("section", "dp"),
            P("section", "dp", None),
            P("section", "dp"),
            P("section", "dp", None),
            P("section", "dp"),
            P("section", "dp"),
            P("section", "dp"),
            P("section", "dp", None),
            P("section", "dp"),
            P("section", "dp", None),
            P("section", "dp"),
        ),
        check_vma=False,
    )
```

profile of v0, /device:TPU:32, one launch (start us, length us, event | category | flops | bytes accessed | tf_op | source)
XLA Modules:
  0.0 1932.3 jit_solution(16708243076042377924)
XLA Ops:
  31.4 346.0 %all-reduce.34 = (bf16[4608]{0:T(1024)(128)(2,1)S(1)}, bf16[1536]{0:T(1024)(128)(2,1)S(1)}, bf16[1536]{0:T(1024)(128)(2,1)S(1)}, bf16[1536]{0:T(1024)(128)(2,1)S...) all-reduce(bf16[4608]{0:T(1024)(128)(2,1)S(1)} %dynamic-update-slic, ...), channel_id=1, replica_groups=mesh['section'=2,'dp'=64] {'dp'}, use_global_device_ids=true, to_apply=%add.20 | all-reduce | flops 19968 | bytes 79872
  394.7 7.8 fusion.504
  404.6 3.4 fusion.770
  408.5 15.6 conditional.6
  408.6 15.3 fusion.8
  428.4 8.7 fusion.507
  441.1 3.4 fusion.772
  445.1 4.0 conditional.7
  445.1 3.6 fusion.176
  450.0 13.9 collective-permute-start.1
  469.0 8.7 fusion.510
  482.5 3.4 fusion.774
  489.4 42.9 %conditional.9 = (f32[64,1536]{1,0:T(8,128)S(1)}, bf16[64,6144]{1,0:T(8,128)(2,1)}, bf16[64,6144]{1,0:T(8,128)(2,1)S(1)}) conditional(s32[]{:T(128)} %clamp.21, (bf16[64,1536]{1,0:T(8,128)(2,1)S(1)}, bf16[6144,1536]{1,0:T(8,128)(2,1)}, bf16[64,1536]{1,0:T(8,128)(2,1)}, bf16[1536,6144]{1,0:T(8,128)(2,1)}, ...), branch_computations={%region_40.41_spmd, %region_41.42_spmd, %region_42.43_spmd, %regio... | conditional | flops 3632928768 | bytes 109738032 | solution.py:173
  489.6 13.3 fusion.784
  502.9 12.0 multiply_convert_fusion
  515.0 9.6 fusion.785
  535.3 4.1 fusion.586
  544.4 10.3 fusion.754
  563.1 48.7 %conditional.10 = (f32[64,1536]{1,0:T(8,128)}, bf16[64,6144]{1,0:T(8,128)(2,1)}, bf16[64,6144]{1,0:T(8,128)(2,1)S(1)}) conditional(s32[]{:T(128)} %clamp.22, (bf16[64,1536]{1,0:T(8,128)(2,1)}, bf16[6144,1536]{1,0:T(8,128)(2,1)}, bf16[64,1536]{1,0:T(8,128)(2,1)}, bf16[1536,6144]{1,0:T(8,128)(2,1)}, ...), branch_computations={%region_55.56_spmd, %region_56.57_spmd, %region_57.58_spmd, %regio... | conditional | flops 3632928768 | bytes 109738032 | solution.py:173
  573.2 13.4 fusion.786
  586.6 12.0 multiply_convert_fusion.4
  598.6 12.9 fusion.787
  611.8 1.9 multiply_reduce_fusion.1
  618.0 4.0 fusion.583
  625.8 2.3 convert_element_type.660
  628.1 10.2 fusion.753
  641.5 2.0 collective-permute-done.3
  644.2 14.5 conditional.11
  649.4 2.4 multiply_convert_fusion.11
  651.8 2.6 fusion.489
  654.4 3.2 fusion.476
  661.2 2.0 fusion.759
  664.2 2.2 copy.135
  667.9 6.2 convolution_bitcast_fusion.3
  676.4 1.9 broadcast_select_fusion.8
  678.3 4.0 fusion.580
  686.2 2.3 convert_element_type.675
  688.5 14.8 convolution_bitcast_fusion.2
  704.3 15.9 convolution_bitcast_fusion.1
  721.5 16.0 convolution_bitcast_fusion
  741.6 3.7 conditional.8
  741.6 3.6 fusion.279
  746.5 9.7 fusion.755
  756.9 344.1 %all-reduce.33 = (f32[1,1536]{1,0:T(1,128)S(1)}, f32[1,1536]{1,0:T(1,128)S(1)}, f32[1,4608]{1,0:T(1,128)S(1)}, f32[1,1536]{1,0:T(1,128)S(1)}, f32[1,1536]{1,0:T(...) all-reduce(f32[1,1536]{1,0:T(1,128)S(1)} %add.1075, ...), channel_id=2, replica_groups=mesh['section'=2,'dp'=64] {'dp'}, use_global_device_ids=true, to_apply=%region_84.85.clone | all-reduce | flops 13824 | bytes 110592
  1107.6 7.9 reduce-scatter.17.cloned.1.call-done
  1115.4 257.8 %reduce-scatter.15.cloned.1.call-done = f32[1,24,4608]{2,1,0:T(8,128)} async-done(((f32[1,1536,4608]{2,1,0:T(8,128)}), f32[1,24,4608]{2,1,0:T(8,128)}) %reduce-scatter.15.cloned.1.call-update) | async-done | bytes 442384 | tf_op jit(solution)/shard_map/reduce_scatter | solution.py:405
  1373.2 275.5 %reduce-scatter.19.cloned.1.call-done = f32[1,24,6144]{2,1,0:T(8,128)} async-done(((f32[1,1536,6144]{2,1,0:T(8,128)}), f32[1,24,6144]{2,1,0:T(8,128)}) %reduce-scatter.19.cloned.1.call-update) | async-done | bytes 589840 | tf_op jit(solution)/shard_map/reduce_scatter | solution.py:411
  1648.7 276.7 %reduce-scatter.21.cloned.1.call-done = f32[1,96,1536]{2,1,0:T(8,128)} async-done(((f32[1,6144,1536]{2,1,0:T(8,128)}), f32[1,96,1536]{2,1,0:T(8,128)}) %reduce-scatter.21.cloned.1.call-update) | async-done | bytes 589840 | tf_op jit(solution)/shard_map/reduce_scatter | solution.py:413
  (637 shorter events, 104.7 us)
Async XLA Ops:
  7.2 387.5 %all-gather.5.cloned.1.call-start = ((), (), s32[]{:S(2)}) async-start(), calls=%async_computation.5 | async-start | bytes 14376960 | tf_op jit(solution)/shard_map/all_gather | solution.py:314
  7.9 396.7 %all-gather.7.cloned.1.call-start = ((), (), s32[]{:S(2)}) async-start(), calls=%async_computation.6 | async-start | bytes 4792320 | tf_op jit(solution)/shard_map/all_gather | solution.py:316
  8.7 399.8 %all-gather.9.cloned.1.call-start = ((), (), s32[]{:S(2)}) async-start(), calls=%async_computation.7 | async-start | bytes 19169280 | tf_op jit(solution)/shard_map/all_gather | solution.py:320
  9.4 399.0 %all-gather.11.cloned.1.call-start = ((), (), s32[]{:S(2)}) async-start(), calls=%async_computation.8 | async-start | bytes 19169280 | tf_op jit(solution)/shard_map/all_gather | solution.py:322
  10.0 1096.2 %reduce-scatter.23.cloned.1.call-start = ((), (), s32[]{:S(2)}) async-start(), calls=%async_computation.13 | async-start | bytes 3194880
  378.0 24.5 %copy-start.114 = (f32[4608]{0:T(1024)}, f32[4608]{0:T(1024)S(1)}, u32[]{:S(2)}) copy-start(f32[4608]{0:T(1024)S(1)} %add.1117) | copy-start | bytes 55300
  378.0 24.5 %copy-start.117 = (f32[1536]{0:T(1024)}, f32[1536]{0:T(1024)S(1)}, u32[]{:S(2)}) copy-start(f32[1536]{0:T(1024)S(1)} %add.1116) | copy-start | bytes 18436
  378.0 24.5 %copy-start.80 = (f32[1536]{0:T(1024)}, f32[1536]{0:T(1024)S(1)}, u32[]{:S(2)}) copy-start(f32[1536]{0:T(1024)S(1)} %mul.2093) | copy-start | bytes 18436
  384.1 18.4 copy-start.176
  394.6 94.7 %copy-start.53 = (bf16[64,1536]{1,0:T(8,128)(2,1)}, bf16[64,1536]{1,0:T(8,128)(2,1)S(1)}, u32[]{:S(2)}) copy-start(bf16[64,1536]{1,0:T(8,128)(2,1)S(1)} %fusion.658) | copy-start | bytes 589828
  403.7 60.1 %copy-start.43 = (bf16[64,12,128]{2,0,1:T(8,128)(2,1)}, bf16[64,12,128]{2,0,1:T(8,128)(2,1)S(1)}, u32[]{:S(2)}) copy-start(bf16[64,12,128]{2,0,1:T(8,128)(2,1)S(1)} %pad_maximum_fusion) | copy-start | bytes 589828
  403.9 60.0 %copy-start.47 = (bf16[64,12,128]{2,0,1:T(8,128)(2,1)}, bf16[64,12,128]{2,0,1:T(8,128)(2,1)S(1)}, u32[]{:S(2)}) copy-start(bf16[64,12,128]{2,0,1:T(8,128)(2,1)S(1)} %pad_maximum_fusion.1) | copy-start | bytes 589828
  408.5 15.7 copy-start.123
  408.5 15.7 copy-start.186
  408.5 17.1 copy-start.192
  408.5 19.9 %copy-start.81 = (f32[1536]{0:T(1024)S(1)}, f32[1536]{0:T(1024)}, u32[]{:S(2)}) copy-start(f32[1536]{0:T(1024)} %copy-done.80) | copy-start | bytes 18436
  408.5 19.9 %copy-start.115 = (f32[4608]{0:T(1024)S(1)}, f32[4608]{0:T(1024)}, u32[]{:S(2)}) copy-start(f32[4608]{0:T(1024)} %copy-done.114) | copy-start | bytes 55300
  408.5 19.9 %copy-start.118 = (f32[1536]{0:T(1024)S(1)}, f32[1536]{0:T(1024)}, u32[]{:S(2)}) copy-start(f32[1536]{0:T(1024)} %copy-done.117) | copy-start | bytes 18436
  424.2 2.4 collective-permute-start
  428.0 37.4 %copy-start.3 = (bf16[64,1536]{1,0:T(8,128)(2,1)}, bf16[64,1536]{1,0:T(8,128)(2,1)S(1)}, u32[]{:S(2)}) copy-start(bf16[64,1536]{1,0:T(8,128)(2,1)S(1)} %get-tuple-element.497) | copy-start | bytes 589828
  440.3 23.6 %copy-start.28 = (bf16[64,12,128]{2,0,1:T(8,128)(2,1)}, bf16[64,12,128]{2,0,1:T(8,128)(2,1)S(1)}, u32[]{:S(2)}) copy-start(bf16[64,12,128]{2,0,1:T(8,128)(2,1)S(1)} %pad_maximum_fusion.2) | copy-start | bytes 589828
  440.5 23.4 %copy-start.32 = (bf16[64,12,128]{2,0,1:T(8,128)(2,1)}, bf16[64,12,128]{2,0,1:T(8,128)(2,1)S(1)}, u32[]{:S(2)}) copy-start(bf16[64,12,128]{2,0,1:T(8,128)(2,1)S(1)} %pad_maximum_fusion.3) | copy-start | bytes 589828
  445.0 18.9 copy-start.163
  445.0 19.9 %copy-start.191 = (f32[64]{0:T(128)S(1)}, f32[64]{0:T(128)}, u32[]{:S(2)}) copy-start(f32[64]{0:T(128)} %get-tuple-element.495) | copy-start | bytes 772
  445.1 23.9 %copy-start.82 = (f32[1536]{0:T(1024)S(1)}, f32[1536]{0:T(1024)}, u32[]{:S(2)}) copy-start(f32[1536]{0:T(1024)} %copy-done.80) | copy-start | bytes 18436
  445.1 23.9 %copy-start.116 = (f32[4608]{0:T(1024)S(1)}, f32[4608]{0:T(1024)}, u32[]{:S(2)}) copy-start(f32[4608]{0:T(1024)} %copy-done.114) | copy-start | bytes 55300
  445.1 23.9 %copy-start.119 = (f32[1536]{0:T(1024)S(1)}, f32[1536]{0:T(1024)}, u32[]{:S(2)}) copy-start(f32[1536]{0:T(1024)} %copy-done.117) | copy-start | bytes 18436
  450.0 18.4 copy-start.104
  450.0 15.5 collective-permute-start.1
  466.8 15.7 copy-start.9
  489.4 44.1 %copy-start.177 = (f32[64]{0:T(128)S(1)}, f32[64]{0:T(128)}, u32[]{:S(2)}) copy-start(f32[64]{0:T(128)} %copy-done.176) | copy-start | bytes 772
  544.3 13.5 copy-start.109
  544.4 14.2 copy-start.108
  555.8 5.1 collective-permute-start.2
  628.1 15.4 copy-start.168
  640.1 3.3 collective-permute-start.3
  644.2 14.5 copy-start.6
  644.2 14.5 copy-start.166
  666.4 449.0 %reduce-scatter.17.cloned.1.call-start = ((), (), s32[]{:S(2)}) async-start(), calls=%async_computation.10 | async-start | bytes 9584640 | tf_op jit(solution)/shard_map/reduce_scatter | solution.py:407
  674.2 699.0 %reduce-scatter.15.cloned.1.call-start = ((), (), s32[]{:S(2)}) async-start(), calls=%async_computation.9 | async-start | bytes 28753920 | tf_op jit(solution)/shard_map/reduce_scatter | solution.py:405
  703.3 945.4 %reduce-scatter.19.cloned.1.call-start = ((), (), s32[]{:S(2)}) async-start(), calls=%async_computation.11 | async-start | bytes 38338560 | tf_op jit(solution)/shard_map/reduce_scatter | solution.py:411
  720.2 1205.2 %reduce-scatter.21.cloned.1.call-start = ((), (), s32[]{:S(2)}) async-start(), calls=%async_computation.12 | async-start | bytes 38338560 | tf_op jit(solution)/shard_map/reduce_scatter | solution.py:413
  746.5 358.6 %copy-start.22 = (f32[64,1536]{1,0:T(8,128)S(1)}, f32[64,1536]{1,0:T(8,128)}, u32[]{:S(2)}) copy-start(f32[64,1536]{1,0:T(8,128)} %get-tuple-element.484) | copy-start | bytes 1179652
  746.5 358.6 %copy-start.74 = (bf16[64,1536]{1,0:T(8,128)(2,1)S(1)}, bf16[64,1536]{1,0:T(8,128)(2,1)}, u32[]{:S(2)}) copy-start(bf16[64,1536]{1,0:T(8,128)(2,1)} %copy-done.72) | copy-start | bytes 589828
  746.5 358.6 %copy-start.107 = (bf16[64,1536]{1,0:T(8,128)(2,1)S(1)}, bf16[64,1536]{1,0:T(8,128)(2,1)}, u32[]{:S(2)}) copy-start(bf16[64,1536]{1,0:T(8,128)(2,1)} %copy-done.106) | copy-start | bytes 589828
  746.5 358.6 %copy-start.170 = (f32[64]{0:T(128)S(1)}, f32[64]{0:T(128)}, u32[]{:S(2)}) copy-start(f32[64]{0:T(128)} %fusion.747) | copy-start | bytes 772
  746.5 358.6 %copy-start.181 = (f32[64]{0:T(128)S(1)}, f32[64]{0:T(128)}, u32[]{:S(2)}) copy-start(f32[64]{0:T(128)} %negate_multiply_fusion.1) | copy-start | bytes 772
  746.5 358.9 %copy-start.111 = (bf16[1,64,1536]{2,1,0:T(8,128)(2,1)S(1)}, bf16[1,64,1536]{2,1,0:T(8,128)(2,1)}, u32[]{:S(2)}) copy-start(bf16[1,64,1536]{2,1,0:T(8,128)(2,1)} %get-tuple-element.478) | copy-start | bytes 589828
  (156 other events, 888.6 us)
Sparse Core Ops, SparseCore 0:
  10.8 97.8 all-gather.4
  111.6 68.9 all-gather.6
  183.5 109.0 all-gather.8
  295.3 110.8 all-gather.10
  666.5 219.4 reduce-scatter.22
  891.0 224.3 reduce-scatter.16
  1121.5 251.6 reduce-scatter.14
  1378.8 269.8 reduce-scatter.18
  1655.1 270.2 reduce-scatter.20
where the time goes:
time: 1940 us; the launch traced here: 1930 us
  waiting for transfers between devices  823 us (42%)
  blocking collectives  690 us (36%)
  matrix products  242 us (12%)
  other arithmetic  64.8 us (3%)
  local copies, waits for them, and re-layouts  37.5 us (2%)
  between operations  32.5 us (2%)
  loops' own time  24.1 us (1%)
    unnamed x2, blocking collectives  690 us
    reduce_scatter x1, waiting for transfers between devices, per_device(): lax.psum_scatter(ffn_totals[4], 'dp', scatter_dimension=1, tiled=True)  277 us
    reduce_scatter x1, waiting for transfers between devices, per_device(): lax.psum_scatter(ffn_totals[2], 'dp', scatter_dimension=1, tiled=True)  276 us
    reduce_scatter x1, waiting for transfers between devices, per_device(): lax.psum_scatter(attention_totals[2], 'dp', scatter_dimension=1, tiled=True)  258 us
  transfers between devices with their start and end apart: 13, of which 6 were waited for; matrix products, arithmetic and copies ran while one was open for 7% of the time, Pallas kernels for 0%

commit v1 on v0

v1 whole, which is shorter than its diff:
```python
import jax
import jax.numpy as jnp
import numpy as np
from jax import lax
from jax.experimental import pallas as pl
from jax.experimental.pallas import tpu as pltpu
from jax.sharding import PartitionSpec as P

MESH = pl.DeviceIdType.MESH
ANY = pl.BlockSpec(memory_space=pl.ANY)
VM = pl.BlockSpec(memory_space=pltpu.VMEM)
EPS = 1e-05
MASKED = -1e9
BF = jnp.bfloat16
F32 = jnp.float32
D = 1536
T = 64
TG = 256
HW = 384
QW = 1152
SCALE = 128 ** -0.5
GC = (2 / np.pi) ** 0.5
PR, OU, EX, SH = range(4)
FULL = ((D, QW), (HW, D), (D, D), (D, D))
SLAB = ((48, QW), (48, HW), (48, D), (96, 768))


def nn(a, b):
    return jnp.dot(a, b, preferred_element_type=F32)


def nt(a, b):
    return lax.dot_general(a, b, (((1,), (1,)), ((), ())), preferred_element_type=F32)


def tn(a, b):
    return lax.dot_general(a, b, (((0,), (0,)), ((), ())), preferred_element_type=F32)


def tiles(count, body):
    def step(i, carry):
        body(i)
        return carry
    lax.fori_loop(0, count, step, 0)


def span(i, size):
    return pl.ds(pl.multiple_of(i * size, size), size)


def at(start, size, unit):
    return pl.ds(pl.multiple_of(start, unit), size)


def stats(x):
    mean = jnp.mean(x, axis=-1, keepdims=True)
    c = x - mean
    var = jnp.mean(c * c, axis=-1, keepdims=True)
    rs = lax.rsqrt(var + EPS)
    return c * rs, rs


def colsum(v):
    return jnp.sum(v, axis=0, keepdims=True)


def to32(v):
    v = v.astype(F32)
    return jnp.concatenate([v, jnp.zeros((8, v.shape[1]), F32)], axis=0).astype(BF)


def core_kernel(h_ref, cot_ref, len_ref, mask_ref, pack_ref, cos_ref, sin_ref, pw, ow, ew, sw,
                act_out, ig_out, sm_out, fp, fo, fe, fs,
                wp, wo, we, ws, r0p, r0o, r0e, r0s, r1p, r1o, r1e, r1s, r2p, r2o, r2e, r2s,
                vp, vo, ve, vs, up, uo, ue, us_,
                normed, ns, gall, dball, qkv, probs, mixed, gder, active, xh1, xh2, rd1, rd2,
                pf, sb, rb, dup, dj, dmix, vis, lens, keep, ostage,
                sp, so, se, cp, co, ce, cs, bp, bo, be, fss,
                tmp, allp, small, smt, sme,
                y_s, y_r, w_sem, x_s, x_r, l_s, l_r, z_s, zo_s, z_r, zs_r, p_s, p_r,
                a_s, a_r, b_s, b_r, c_s, c_r, o_sem, q0_s, q0_r, q1_s, q1_r, q2_s, q2_r, t_sem,
                f_s, f_r, e_s, e_r):
    s = lax.axis_index("section")
    chip = lax.axis_index("dp")
    y, x, z = chip // 16, (chip // 4) % 4, chip % 4
    t = y
    zp = z % 2
    zh = z // 2
    first = s == 0

    def dev(core, cy, cx, cz):
        return (core, cy * 16 + cx * 4 + cz)

    def ypeer(d):
        return dev(s, (y + d) % 4, x, z)

    a_me = jnp.where(first, x, z)
    b_me = jnp.where(first, z, x)

    def grid(a, b):
        return jnp.where(first, a, b), jnp.where(first, b, a)

    def apeer(d):
        cx, cz = grid((a_me + d) % 4, b_me)
        return dev(s, y, cx, cz)

    def bpeer(d):
        cx, cz = grid(a_me, (b_me + d) % 4)
        return dev(s, y, cx, cz)

    sib = dev(1 - s, y, x, z)
    own = at(t * T, T, T)

    bar = pltpu.get_barrier_semaphore()

    def greet(who):
        pl.semaphore_signal(bar, inc=1, device_id=who, device_id_type=MESH)

    for d in (1, 2, 3):
        for core in (s, 1 - s):
            greet(dev(core, (y + d) % 4, x, z))
    for d in (0, 1, 2, 3):
        for core in (s, 1 - s):
            greet(dev(core, (y + d) % 4, x, 2 * zh + 1 - zp))
    greet(sib)
    for d in (1, 2, 3):
        greet(dev(s, y, (x + d) % 4, z))
    for d in (0, 1):
        greet(dev(s, y, x, 2 * (1 - zh) + d))
    pl.semaphore_wait(bar, 20)

    def remote(src, dst, ssem, rsem, who):
        return pltpu.make_async_remote_copy(src_ref=src, dst_ref=dst, send_sem=ssem, recv_sem=rsem,
                                            device_id=who, device_id_type=MESH)

    def wait_for(ref, sem):
        pltpu.make_async_copy(ref, ref, sem).wait()

    w_hbm = (wp, wo, we, ws)
    w_v = (vp, vo, ve, vs)
    g_v = (up, uo, ue, us_)
    r0 = (r0p, r0o, r0e, r0s)
    r1 = (r1p, r1o, r1e, r1s)
    r2 = (r2p, r2o, r2e, r2s)

    def slab_at(k, j, cx, cz):
        if k in (PR, EX):
            return at(48 * (8 * (2 * (cz % 2) + j) + 2 * cx + cz // 2), 48, 48), slice(None)
        if k == OU:
            return at(48 * (2 * cx + cz // 2), 48, 48), at(HW * (2 * (cz % 2) + j), HW, HW)
        return at(96 * (4 * cx + cz), 96, 96), at(768 * j, 768, 768)

    def slab_of(ref, k, a, b):
        cx, cz = grid(a, b)
        return ref.at[slab_at(k, s, cx, cz)]

    def parts_of(ref, k, j):
        if k in (PR, EX):
            return [ref.at[at(HW * (2 * p + j), HW, HW)] for p in (0, 1)]
        if k == OU:
            return [ref.at[:, at(HW * (2 * p + j), HW, HW)] for p in (0, 1)]
        return [ref.at[:, at(768 * j, 768, 768)]]

    def bulk(ref, k, slabs):
        if k in (PR, EX):
            return ref.at[pl.ds(0, 48 * slabs)]
        if k == OU:
            return ref.at[pl.ds(0, 12 * slabs)] if slabs > 3 else ref.at[pl.ds(0, 144), pl.ds(0, HW)]
        return ref.at[pl.ds(0, 48 * slabs)]

    def piece_target(yt):
        return dev(y % 2, yt, x, 2 * zh + y // 2), (yt == y) & (s == y % 2) & (zp == y // 2)

    def out_target(q):
        return dev(q % 2, y, x, 2 * zh + q // 2), (zp == q // 2) & (s == q % 2)

    def send_or_keep(src, dst, ssem, rsem, who, is_me):
        @pl.when(is_me)
        def _():
            pltpu.make_async_copy(src, dst, rsem).start()

        @pl.when(jnp.logical_not(is_me))
        def _():
            remote(src, dst, ssem, rsem, who).start()

    def sent(src, dst, ssem, rsem, who, is_me):
        @pl.when(jnp.logical_not(is_me))
        def _():
            remote(src, dst, ssem, rsem, who).wait_send()

    def shard_moves():
        out = []
        for yt in range(4):
            who, me = piece_target(yt)
            out.append((sp.at[yt], cp.at[s, zp], z_s.at[0, yt], z_r.at[0, s, zp], who, me))
        for q in range(4):
            who, me = out_target(q)
            out.append((so.at[q], co.at[s, zp], z_s.at[1, q], z_r.at[1, s, zp], who, me))
        for yt in range(4):
            who, me = piece_target(yt)
            out.append((se.at[yt], ce.at[s, zp], z_s.at[2, yt], z_r.at[2, s, zp], who, me))
        for j in range(2):
            out.append((sw.at[0, :, pl.ds(768 * j, 768)], cs.at[s], zo_s.at[j], zs_r.at[s],
                        dev(j, y, x, z), s == j))
        return out

    moves = shard_moves()
    for yt in range(4):
        sp[yt] = to32(jnp.concatenate([pw[0, :, p * D + HW * yt:p * D + HW * (yt + 1)] for p in range(3)], axis=1))
    for m in moves[:4]:
        send_or_keep(*m)
    for q in range(4):
        so[q] = to32(ow[0, :, HW * q:HW * (q + 1)])
    for m in moves[4:8]:
        send_or_keep(*m)
    for yt in range(4):
        se[yt] = to32(ew[0, :, D * yt:D * (yt + 1)])
    for m in moves[8:]:
        send_or_keep(*m)

    allp[s, pl.ds(chip, 1)] = pack_ref[...][None]

    def pack_copies(stage):
        out = []
        for d in (1, 2, 3):
            if stage == 0:
                blk, who = allp.at[s, pl.ds(chip, 1)], dev(s, y, x, (z + d) % 4)
            elif stage == 1:
                blk, who = allp.at[s, at(chip - z, 4, 4)], dev(s, y, (x + d) % 4, z)
            else:
                blk, who = allp.at[s, at(16 * y, 16, 16)], ypeer(d)
            out.append(remote(blk, blk, p_s.at[stage, d - 1], p_r.at[stage, d - 1], who))
        return out

    def pack_go(stage):
        for c in pack_copies(stage):
            c.start()

    def pack_end(stage):
        for c in pack_copies(stage):
            c.wait()

    pack_go(0)

    lens[pl.ds(t, 1)] = len_ref[...][None]
    lcs = []
    for d in (1, 2, 3):
        c = remote(lens.at[pl.ds(t, 1)], lens.at[pl.ds(t, 1)], l_s.at[d - 1], l_r.at[d - 1], ypeer(d))
        c.start()
        lcs.append(c)

    got = (cp, co, ce, cs)
    bld = (bp, bo, be, cs)

    def a_copies(l, k):
        src = bld[k].at[l]
        return [remote(src, slab_of(w_hbm[k].at[l], k, a_me, b_me), a_s.at[l, k], a_r.at[l, k], apeer(d))
                for d in (1, 2, 3)]

    def own_copy(l, k):
        return pltpu.make_async_copy(bld[k].at[l], slab_of(w_hbm[k].at[l], k, a_me, b_me), o_sem.at[l, k])

    def gather_a(l, k):
        if k == SH:
            wait_for(cs.at[l], zs_r.at[l])
        else:
            zk = (0, 1, 2)[k]
            for p in (0, 1):
                wait_for(got[k].at[l, p], z_r.at[zk, l, p])
            halves = [got[k][l, p].astype(F32)[:24] for p in (0, 1)]
            bld[k][l] = jnp.concatenate(halves, axis=0).astype(BF)
        for c in a_copies(l, k):
            c.start()
        own_copy(l, k).start()

    def gather_b(l, k):
        w = w_hbm[k].at[l]
        wait_for(bulk(w, k, 3), a_r.at[l, k])
        own_copy(l, k).wait()
        for da in (0, 1, 2, 3):
            src = slab_of(w, k, (a_me + da) % 4, b_me)
            for d in (1, 2, 3):
                remote(src, src, b_s.at[l, k], b_r.at[l, k], bpeer(d)).start()

    def gather_c(l, k):
        w = w_hbm[k].at[l]
        wait_for(bulk(w, k, 12), b_r.at[l, k])
        for blk in parts_of(w, k, s):
            remote(blk, blk, c_s.at[l, k], c_r.at[l, k], sib).start()

    def gather_d(l, k):
        wait_for(bulk(w_hbm[k].at[l], k, 16), c_r.at[l, k])

    def gather_drain(l, k):
        w = w_hbm[k].at[l]
        wait_for(bulk(w, k, 3), a_s.at[l, k])
        wait_for(bulk(w, k, 12), b_s.at[l, k])
        wait_for(bulk(w, k, 16), c_s.at[l, k])

    def sum0_go(l, k):
        for i, blk in enumerate(parts_of(g_v[k], k, 1 - s)):
            dst = r0[k].at[l, i] if k != SH else r0[k].at[l]
            remote(blk, dst, q0_s.at[l, k], q0_r.at[l, k], sib).start()

    def halves_tmp(k):
        if k in (PR, EX):
            return [tmp.at[pl.ds(HW * p, HW), pl.ds(0, FULL[k][1])] for p in (0, 1)]
        if k == OU:
            return [tmp.at[pl.ds(HW * p, HW), pl.ds(0, HW)] for p in (0, 1)]
        return [tmp.at[:, pl.ds(768 * p, 768)] for p in (0, 1)]

    def sum0_end(l, k):
        wait_for(r0[k].at[l], q0_r.at[l, k])
        srcs = [r0[k].at[l, i] for i in (0, 1)] if k != SH else [r0[k].at[l, pl.ds(768 * i, 768)] for i in (0, 1)]
        cps = [pltpu.make_async_copy(a, b, t_sem.at[i]) for i, (a, b) in enumerate(zip(srcs, halves_tmp(k)))]
        for c in cps:
            c.start()
        for p in (0, 1):
            cps[p].wait()

            def add(i):
                if k in (PR, EX):
                    rows, cols, n = at(HW * (2 * p + s) + 96 * i, 96, 96), slice(None), FULL[k][1]
                    other = tmp[pl.ds(pl.multiple_of(HW * p + 96 * i, 96), 96), 0:n]
                elif k == OU:
                    rows, cols = span(i, 96), at(HW * (2 * p + s), HW, HW)
                    other = tmp[pl.ds(pl.multiple_of(HW * p + 96 * i, 96), 96), 0:HW]
                else:
                    rows, cols = at(768 * p + 96 * i, 96, 96), at(768 * s, 768, 768)
                    other = tmp[span(i, 96), 768 * p:768 * p + 768]
                g_v[k][rows, cols] = (g_v[k][rows, cols].astype(F32) + other.astype(F32)).astype(BF)
            tiles(8 if k == SH else 4, add)
        for d in (1, 2, 3):
            for da in (0, 1, 2, 3):
                a = (a_me + da) % 4
                remote(slab_of(g_v[k], k, a, (b_me + d) % 4), r1[k].at[l, d - 1, da],
                       q1_s.at[l, k], q1_r.at[l, k], bpeer(d)).start()

    def tmp_slab(k, i):
        rows, cols = SLAB[k]
        if k == SH:
            return pl.ds(rows * (i % 6), rows), pl.ds(768 * (i // 6), 768)
        return pl.ds(rows * i, rows), pl.ds(0, cols)

    def sum1_end(l, k):
        wait_for(r1[k].at[l], q1_r.at[l, k])
        cps = []
        for d in range(3):
            for da in range(4):
                c = pltpu.make_async_copy(r1[k].at[l, d, da], tmp.at[tmp_slab(k, d * 4 + da)], t_sem.at[2 + d * 4 + da])
                c.start()
                cps.append(c)
        for c in cps:
            c.wait()
        for da in (1, 2, 3, 0):
            cx, cz = grid((a_me + da) % 4, b_me)
            where = slab_at(k, s, cx, cz)
            total = g_v[k][where].astype(F32)
            for d in range(3):
                total = total + tmp[tmp_slab(k, d * 4 + da)].astype(F32)
            if da == 0:
                bld[k][l] = total.astype(BF)
            else:
                g_v[k][where] = total.astype(BF)
                remote(slab_of(g_v[k], k, (a_me + da) % 4, b_me), r2[k].at[l, da - 1],
                       q2_s.at[l, k], q2_r.at[l, k], apeer(da)).start()

    fsend = (sp, so, se, fss)
    frecv = (fp, fo, fe, fs)

    def last_moves(l, k):
        out = []
        if k == SH:
            out.append((fss.at[l], fs.at[s], f_s.at[l, k, 0], f_r.at[k, s], dev(l, y, x, z), s == l))
            return out
        for p in (0, 1):
            if k == OU:
                q = 2 * zp + s
                who, me, slot = dev(l, y, x, 2 * zh + p), (s == l) & (zp == p), q
            else:
                yo = 2 * zp + s
                who, me, slot = dev(l, yo, x, 2 * zh + p), (s == l) & (yo == y) & (zp == p), y
            out.append((fsend[k].at[2 * l + p], frecv[k].at[slot], f_s.at[l, k, p], f_r.at[k, slot], who, me))
        return out

    def sum2_end(l, k):
        wait_for(r2[k].at[l], q2_r.at[l, k])
        cps = []
        for d in range(3):
            c = pltpu.make_async_copy(r2[k].at[l, d], tmp.at[tmp_slab(k, d)], t_sem.at[2 + d])
            c.start()
            cps.append(c)
        for c in cps:
            c.wait()
        total = bld[k][l].astype(F32)
        for d in range(3):
            total = total + tmp[tmp_slab(k, d)].astype(F32)
        if k == SH:
            fss[l] = total.astype(BF)
        else:
            for p in (0, 1):
                fsend[k][2 * l + p] = to32(total[24 * p:24 * (p + 1)])
        for m in last_moves(l, k):
            send_or_keep(*m)

    def sum_drain(l, k):
        wait_for(r0[k].at[l], q0_s.at[l, k])
        wait_for(r1[k].at[l], q1_s.at[l, k])
        wait_for(r2[k].at[l], q2_s.at[l, k])

    def finish_weights():
        for l in (0, 1):
            for k in range(4):
                for m in last_moves(l, k):
                    sent(*m)
        for k in range(4):
            for i in range(2 if k == SH else 4):
                wait_for(frecv[k].at[i], f_r.at[k, i])

    def vec_copies(stage):
        out = []
        if stage == 0:
            out.append(remote(smt.at[1 - s], sme.at[0, 0], e_s.at[0, 0], e_r.at[0, 0], sib))
            return out
        for d in (1, 2, 3):
            if stage == 1:
                who = dev(s, y, x, (z + d) % 4)
            elif stage == 2:
                who = dev(s, y, (x + d) % 4, z)
            else:
                out.append(remote(sm_out.at[t], sm_out.at[t], e_s.at[3, d - 1], e_r.at[3, d - 1], ypeer(d)))
                continue
            out.append(remote(smt.at[2 + stage], sme.at[stage, d - 1], e_s.at[stage, d - 1], e_r.at[stage, d - 1], who))
        return out

    def vec_go(stage):
        for c in vec_copies(stage):
            c.start()

    def vec_end(stage):
        for c in vec_copies(stage):
            c.wait()
        if stage == 0:
            smt[3] = smt[pl.ds(s, 1)][0] + sme[0, 0]
        elif stage == 1:
            smt[4] = smt[3] + sme[1, 0] + sme[1, 1] + sme[1, 2]
        elif stage == 2:
            sm_out[pl.ds(t, 1)] = (smt[4] + sme[2, 0] + sme[2, 1] + sme[2, 2])[None]

    def wcopy(k, l):
        return pltpu.make_async_copy(w_hbm[k].at[l], w_v[k], w_sem.at[k])

    def ag_copies(buf, idx):
        return [remote(buf.at[own], buf.at[own], y_s.at[idx, d - 1], y_r.at[idx, d - 1], ypeer(d)) for d in (1, 2, 3)]

    def go(cps):
        for c in cps:
            c.start()

    def end(cps):
        for c in cps:
            c.wait()

    def reduce_go(idx):
        cps = []
        for d in (1, 2, 3):
            r = (t + d) % 4
            sb[d - 1] = pf[at(r * T, T, T), :].astype(BF)
            c = remote(sb.at[d - 1], rb.at[idx % 2, d - 1], y_s.at[8 + idx, d - 1], y_r.at[8 + idx, d - 1], ypeer(d))
            c.start()
            cps.append(c)
        return cps

    def reduce_end(cps, idx):
        end(cps)
        total = pf[own, :]
        for d in (1, 2, 3):
            total = total + rb[idx % 2, d - 1].astype(F32)
        return total

    live = lax.broadcasted_iota(jnp.int32, (T, 128), 0).astype(F32) < len_ref[0:1, :]
    livef = jnp.concatenate([jnp.where(live, 1.0, 0.0)] * 12, axis=1)

    def put_result(l, ref, value, way):
        @pl.when(s == l)
        def _():
            ref[pl.ds(s, 1)] = value[None]

        @pl.when(s != l)
        def _():
            ostage[way] = value
            remote(ostage.at[way], ref.at[s], x_s.at[way], x_r.at[way], sib).start()

    def finish_results():
        for way, ref in enumerate((act_out, ig_out)):
            remote(ostage.at[way], ref.at[s], x_s.at[way], x_r.at[way], sib).wait()

    def nothing():
        pass

    def forward(l, hidden, hooks):
        hook = lambda name: hooks.get(name, nothing)()
        xh, rsd = stats(hidden)
        xh1[l] = xh
        rd1[l] = jnp.broadcast_to(rsd, (T, 128))
        normed[l, own, :] = (xh * small[l, 0:1, :] + small[l, 1:2, :]).astype(BF)
        cps = ag_copies(normed.at[l], l * 2)
        go(cps)
        hook("normed")
        end(cps)
        wcopy(PR, l).wait()
        for part in range(3):
            joined = nn(normed[l], vp[:, part * HW:(part + 1) * HW]) + small[l, 7:8, part * HW:(part + 1) * HW]
            for h in range(3):
                v = joined[:, h * 128:(h + 1) * 128]
                if part < 2:
                    v = v * cos_ref[...] + pltpu.roll(v, 64, 1) * sin_ref[...]
                qkv[l, :, part * HW + h * 128:part * HW + (h + 1) * 128] = v.astype(BF)
        hook("joined")
        for h in range(3):
            q = qkv[l, :, h * 128:(h + 1) * 128]
            k = qkv[l, :, HW + h * 128:HW + (h + 1) * 128]
            v = qkv[l, :, 2 * HW + h * 128:2 * HW + (h + 1) * 128]
            sc = jnp.where(vis[...] > 0.5, nt(q, k) * SCALE, MASKED)
            top = jnp.max(sc, axis=-1, keepdims=True)
            ex = jnp.exp(sc - top)
            p = ex * (1.0 / jnp.sum(ex, axis=-1, keepdims=True))
            probs[l, h] = p
            mixed[l, :, h * 128:(h + 1) * 128] = nn(p.astype(BF), v).astype(BF)
        wcopy(OU, l).wait()

        def out_tile(i):
            pf[:, span(i, 512)] = nn(mixed[l], vo[:, span(i, 512)])
        tiles(3, out_tile)
        cps = reduce_go(l * 2)
        hook("mixed")
        middle = hidden + reduce_end(cps, l * 2) + small[l, 2:3, :]
        xh, rsd = stats(middle)
        xh2[l] = xh
        rd2[l] = jnp.broadcast_to(rsd, (T, 128))
        ns[l, own, :] = (xh * small[l, 3:4, :] + small[l, 4:5, :]).astype(BF)
        keep[...] = middle
        cps = ag_copies(ns.at[l], l * 2 + 1)
        go(cps)
        hook("second")
        end(cps)
        wcopy(EX, l).wait()

        def up_tile(i):
            c = span(i, 256)
            u = nn(ns[l], ve[:, c]) + small[l, 6:7, c]
            m = mask_ref[0:1, c]
            u2 = u * u
            th = jnp.tanh(GC * u * (1.0 + 0.044715 * u2))
            half = 0.5 * (1.0 + th)
            active[l, :, c] = (u * half * m).astype(BF)
            gder[l, :, c] = m * (half + 0.5 * u * (1.0 - th * th) * (GC * (1.0 + 3 * 0.044715 * u2)))
        tiles(6, up_tile)
        hook("upper")
        wcopy(SH, l).wait()

        def down_tile(i):
            pf[:, span(i, 256)] = nn(active[l], vs[:, span(i, 256)])
        tiles(6, down_tile)
        cps = reduce_go(l * 2 + 1)
        hook("down")
        result = (keep[...] + reduce_end(cps, l * 2 + 1) + small[l, 5:6, :]) * livef
        result = result.astype(BF)
        put_result(l, act_out, result, 0)
        return result

    def norm_back(dn, xh, rsd, gain):
        e = dn * gain
        return rsd[:, 0:1] * (e - jnp.mean(e, axis=-1, keepdims=True)
                              - xh * jnp.mean(e * xh, axis=-1, keepdims=True))

    def backward(l, g, hooks):
        hook = lambda name: hooks.get(name, nothing)()
        g32 = g.astype(F32)
        smt[l, 5:6, :] = colsum(g32)
        gall[own, :] = g
        cps = ag_copies(gall, 4 + l * 2)
        go(cps)
        hook("grad")
        end(cps)
        if l == 0:
            wcopy(SH, 0).wait()

        def dact_tile(i):
            c = span(i, 256)
            da = nt(gall[...], vs[c, :]) * gder[l, :, c]
            da = da.astype(BF)
            dup[:, c] = da
            smt[l, 6:7, c] = colsum(da.astype(F32))
        tiles(6, dact_tile)
        if l == 1:
            wcopy(SH, 0).start()
        else:
            wcopy(EX, 0).wait()

        def e_tile(i):
            c = span(i, 256)
            pf[:, c] = nt(dup[...], ve[c, :])
        tiles(6, e_tile)
        if l == 1:
            wcopy(EX, 0).start()
        cps = reduce_go(4 + l * 2)
        hook("upper")

        def gs_tile(i):
            c = span(i, 256)
            us_[c, :] = tn(active[l, :, c], gall[...]).astype(BF)
        tiles(6, gs_tile)
        sum0_go(l, SH)
        dn = reduce_end(cps, 4 + l * 2)
        smt[l, 3:4, :] = colsum(dn * xh2[l])
        smt[l, 4:5, :] = colsum(dn)
        dmid = g32 + norm_back(dn, xh2[l], rd2[l], small[l, 3:4, :])
        db = dmid.astype(BF)
        smt[l, 2:3, :] = colsum(db.astype(F32))
        keep[...] = dmid
        dball[own, :] = db
        cps = ag_copies(dball, 4 + l * 2 + 1)
        go(cps)

        def ge_tile(i):
            c = span(i, 256)
            ue[c, :] = tn(ns[l, :, c], dup[...]).astype(BF)
        tiles(6, ge_tile)
        sum0_go(l, EX)
        hook("middle")
        end(cps)
        if l == 0:
            wcopy(OU, 0).wait()
        dmix[...] = nt(dball[...], vo[...]).astype(BF)
        if l == 1:
            wcopy(OU, 0).start()
        for h in range(3):
            c = slice(h * 128, (h + 1) * 128)
            q = qkv[l, :, h * 128:(h + 1) * 128]
            k = qkv[l, :, HW + h * 128:HW + (h + 1) * 128]
            v = qkv[l, :, 2 * HW + h * 128:2 * HW + (h + 1) * 128]
            p = probs[l, h]
            dm = dmix[:, c]
            dj[:, 2 * HW + h * 128:2 * HW + (h + 1) * 128] = tn(p.astype(BF), dm).astype(BF)
            dp = nt(dm, v)
            dsc = (p * (dp - jnp.sum(dp * p, axis=-1, keepdims=True))).astype(BF)
            for part, v in ((0, nn(dsc, k)), (1, tn(dsc, q))):
                v = v * SCALE
                v = v * cos_ref[...] - pltpu.roll(v, 64, 1) * sin_ref[...]
                dj[:, part * HW + h * 128:part * HW + (h + 1) * 128] = v.astype(BF)
        smt[l, 7:8, :] = jnp.zeros((1, D), F32)
        smt[l, 7:8, 0:QW] = colsum(dj[...].astype(F32))
        if l == 0:
            wcopy(PR, 0).wait()

        def d_tile(i):
            c = span(i, 256)
            pf[:, c] = nt(dj[...], vp[c, :])
        tiles(6, d_tile)
        if l == 1:
            wcopy(PR, 0).start()
        cps = reduce_go(4 + l * 2 + 1)
        hook("joined")
        uo[...] = tn(mixed[l], dball[...]).astype(BF)
        sum0_go(l, OU)

        def gp_tile(i):
            c = span(i, 256)
            up[c, :] = tn(normed[l, :, c], dj[...]).astype(BF)
        tiles(6, gp_tile)
        sum0_go(l, PR)
        hook("project")
        dn = reduce_end(cps, 4 + l * 2 + 1)
        smt[l, 0:1, :] = colsum(dn * xh1[l])
        smt[l, 1:2, :] = colsum(dn)
        dh = keep[...] + norm_back(dn, xh1[l], rd1[l], small[l, 0:1, :])
        res = dh.astype(BF)
        put_result(l, ig_out, res, 1)
        return res

    gather_a(0, PR)
    gather_a(0, OU)
    pack_end(0)
    pack_go(1)
    gather_a(0, EX)
    gather_a(0, SH)
    gather_b(0, PR)
    pack_end(1)
    pack_go(2)
    gather_b(0, OU)
    gather_b(0, EX)
    gather_b(0, SH)
    pack_end(2)
    pltpu_pack = remote(allp.at[s], allp.at[s], p_s.at[3, 0], p_r.at[3, 0], sib)
    pltpu_pack.start()
    gather_c(0, PR)
    end(lcs)
    row = lax.broadcasted_iota(jnp.int32, (TG, TG), 0)
    col = lax.broadcasted_iota(jnp.int32, (TG, TG), 1)
    limit = jnp.zeros((1, TG), F32)
    blk = lax.broadcasted_iota(jnp.int32, (1, TG), 1) // T
    for r in range(4):
        one = lens[r][0:1, :]
        limit = jnp.where(blk == r, jnp.concatenate([one, one], axis=1), limit)
    ok = (row // T == col // T) & (col <= row) & ((col % T).astype(F32) < limit)
    vis[...] = jnp.where(ok, 1.0, 0.0)
    pltpu_pack.wait()

    def spread(rows, width, total):
        n = lax.broadcasted_iota(jnp.int32, (128, total), 1)
        i = lax.broadcasted_iota(jnp.int32, (128, total), 0)
        pick = jnp.where(n - (n // width) * width == i, 1.0, 0.0).astype(BF)
        wide = nn(rows.astype(BF), pick)
        n = lax.broadcasted_iota(jnp.int32, (64, total), 1)
        c = lax.broadcasted_iota(jnp.int32, (64, total), 0)
        return colsum(jnp.where(n // width == c, wide, 0.0))

    for l in (0, 1):
        for r in range(6):
            small[l, r:r + 1, :] = spread(allp[l, :, r, :], 24, D)
        mine = allp[l, at(16 * t, 16, 16), 6, :]
        n = lax.broadcasted_iota(jnp.int32, (128, D), 1)
        i = lax.broadcasted_iota(jnp.int32, (128, D), 0)
        pick = jnp.where(n - (n // 96) * 96 == i, 1.0, 0.0).astype(BF)
        wide = nn(mine.astype(BF), pick)
        n = lax.broadcasted_iota(jnp.int32, (16, D), 1)
        c = lax.broadcasted_iota(jnp.int32, (16, D), 0)
        small[l, 6:7, :] = colsum(jnp.where(n // 96 == c, wide, 0.0))
        n = lax.broadcasted_iota(jnp.int32, (128, QW), 1)
        i = lax.broadcasted_iota(jnp.int32, (128, QW), 0)
        n = n + (n // HW) * (D - HW) + HW * t
        pick = jnp.where(n - (n // 72) * 72 == i, 1.0, 0.0).astype(BF)
        wide = nn(allp[l, :, 7, :].astype(BF), pick)
        n = lax.broadcasted_iota(jnp.int32, (64, QW), 1)
        c = lax.broadcasted_iota(jnp.int32, (64, QW), 0)
        n = n + (n // HW) * (D - HW) + HW * t
        small[l, 7:8, 0:QW] = colsum(jnp.where(n // 72 == c, wide, 0.0))

    def f0_normed():
        gather_d(0, PR)
        wcopy(PR, 0).start()
        gather_c(0, OU)

    def f0_joined():
        for k in range(4):
            gather_a(1, k)
        gather_d(0, OU)
        wcopy(OU, 0).start()

    def f0_mixed():
        gather_c(0, EX)
        gather_b(1, PR)
        gather_b(1, OU)

    def f0_second():
        gather_d(0, EX)
        wcopy(EX, 0).start()
        gather_c(0, SH)
        gather_b(1, EX)
        gather_b(1, SH)

    def f0_upper():
        gather_d(0, SH)
        wcopy(SH, 0).start()
        gather_c(1, PR)

    def f0_down():
        gather_d(1, PR)
        wcopy(PR, 1).start()
        gather_c(1, OU)

    def f1_normed():
        gather_d(1, OU)
        wcopy(OU, 1).start()

    def f1_mixed():
        gather_c(1, EX)

    def f1_second():
        gather_d(1, EX)
        wcopy(EX, 1).start()
        gather_c(1, SH)

    def f1_upper():
        gather_d(1, SH)
        wcopy(SH, 1).start()

    h0 = h_ref[...].astype(F32)
    a1 = forward(0, h0, dict(normed=f0_normed, joined=f0_joined, mixed=f0_mixed, second=f0_second,
                             upper=f0_upper, down=f0_down))
    forward(1, a1.astype(F32), dict(normed=f1_normed, mixed=f1_mixed, second=f1_second, upper=f1_upper))

    for k in range(4):
        for l in (0, 1):
            gather_drain(l, k)
    for m in moves:
        sent(*m)

    def b1_middle():
        sum0_end(1, SH)

    def b1_joined():
        sum0_end(1, EX)

    def b0_grad():
        sum0_end(1, OU)
        sum0_end(1, PR)

    def b0_upper():
        sum1_end(1, SH)
        sum1_end(1, EX)
        sum_drain(1, SH)
        sum_drain(1, EX)

    def b0_middle():
        sum0_end(0, SH)
        sum1_end(1, OU)
        sum1_end(1, PR)

    def b0_joined():
        sum0_end(0, EX)
        sum2_end(1, SH)
        sum2_end(1, EX)
        sum_drain(1, OU)
        sum_drain(1, PR)

    g2 = (cot_ref[...].astype(F32) * livef).astype(BF)
    ig2 = backward(1, g2, dict(middle=b1_middle, joined=b1_joined))
    g1 = (ig2.astype(F32) * livef).astype(BF)
    backward(0, g1, dict(grad=b0_grad, upper=b0_upper, middle=b0_middle, joined=b0_joined))
    vec_go(0)
    sum0_end(0, OU)
    sum0_end(0, PR)
    vec_end(0)
    vec_go(1)
    sum1_end(0, SH)
    sum1_end(0, EX)
    vec_end(1)
    vec_go(2)
    sum2_end(1, OU)
    sum2_end(1, PR)
    vec_end(2)
    vec_go(3)
    sum1_end(0, OU)
    sum1_end(0, PR)
    for k in (SH, EX, OU, PR):
        sum2_end(0, k)
    vec_end(3)
    finish_weights()
    finish_results()
    for k in range(4):
        sum_drain(0, k)


def core_call(h, cot, lens, mask, pack, cos2, sin2, pw, ow, ew, sw):
    sd = jax.ShapeDtypeStruct
    V = pltpu.VMEM
    DMA = pltpu.SemaphoreType.DMA
    hbm = [sd((2,) + f, BF) for f in FULL]
    hbm += [sd((2, 2, HW, QW), BF), sd((2, 2, HW, HW), BF), sd((2, 2, HW, D), BF), sd((2, D, 768), BF)]
    hbm += [sd((2, 3, 4) + f, BF) for f in SLAB]
    hbm += [sd((2, 3) + f, BF) for f in SLAB]
    out = pl.pallas_call(
        core_kernel,
        out_shape=[sd((2, T, D), BF), sd((2, T, D), BF), sd((4, 8, D), F32),
                   sd((4, 32, QW), BF), sd((4, 32, HW), BF), sd((4, 32, D), BF), sd((2, 96, 768), BF)] + hbm,
        in_specs=[VM] * 11,
        out_specs=[VM] * 7 + [ANY] * 16,
        scratch_shapes=[
            V((D, QW), BF), V((HW, D), BF), V((D, D), BF), V((D, D), BF),
            V((D, QW), BF), V((HW, D), BF), V((D, D), BF), V((D, D), BF),
            V((2, TG, D), BF), V((2, TG, D), BF), V((TG, D), BF), V((TG, D), BF),
            V((2, TG, QW), BF), V((2, 3, TG, TG), F32), V((2, TG, HW), BF),
            V((2, TG, D), F32), V((2, TG, D), BF),
            V((2, T, D), F32), V((2, T, D), F32), V((2, T, 128), F32), V((2, T, 128), F32),
            V((TG, D), F32), V((3, T, D), BF), V((2, 3, T, D), BF),
            V((TG, D), BF), V((TG, QW), BF), V((TG, HW), BF), V((TG, TG), F32), V((4, 8, 128), F32),
            V((T, D), F32), V((2, T, D), BF),
            V((4, 32, QW), BF), V((4, 32, HW), BF), V((4, 32, D), BF),
            V((2, 2, 32, QW), BF), V((2, 2, 32, HW), BF), V((2, 2, 32, D), BF), V((2, 96, 768), BF),
            V((2, 48, QW), BF), V((2, 48, HW), BF), V((2, 48, D), BF),
            V((2, 96, 768), BF),
            V((768, D), BF), V((2, 64, 8, 128), F32), V((2, 8, D), F32), V((5, 8, D), F32), V((3, 3, 8, D), F32),
            DMA((16, 3)), DMA((16, 3)), DMA((4,)), DMA((4,)), DMA((4,)), DMA((3,)), DMA((3,)),
            DMA((3, 4)), DMA((2,)), DMA((3, 2, 2)), DMA((2,)), DMA((4, 3)), DMA((4, 3)),
            DMA((2, 4)), DMA((2, 4)), DMA((2, 4)), DMA((2, 4)), DMA((2, 4)), DMA((2, 4)), DMA((2, 4)),
            DMA((2, 4)), DMA((2, 4)), DMA((2, 4)), DMA((2, 4)), DMA((2, 4)), DMA((2, 4)), DMA((14,)),
            DMA((2, 4, 2)), DMA((4, 4)), DMA((4, 3)), DMA((4, 3)),
        ],
        compiler_params=pltpu.CompilerParams(collective_id=1, has_side_effects=True,
                                             vmem_limit_bytes=64 * 2**20 - 2**16),
    )(h, cot, lens, mask, pack, cos2, sin2, pw, ow, ew, sw)
    return out[:7]


def rotary():
    half = 64
    rates = (np.float32(10000.0) ** (-np.arange(half, dtype=np.float32) / np.float32(half))).astype(np.float32)
    ang = np.arange(T, dtype=np.float32)[:, None] * rates[None, :]
    cos, sin = np.cos(ang), np.sin(ang)
    cos2 = np.concatenate([cos, cos], axis=1)
    sin2 = np.concatenate([-sin, sin], axis=1)
    return np.tile(cos2, (4, 1)).astype(np.float32), np.tile(sin2, (4, 1)).astype(np.float32)


def per_device(window_input, cotangent, lengths, widths, gain_first, shift_first, project_weight, project_bias,
               output_weight, output_bias, gain_second, shift_second, expand_weight, expand_bias,
               shrink_weight, shrink_bias):
    s = lax.axis_index("section")
    chip = lax.axis_index("dp")
    t = chip // 16
    vectors = (gain_first, shift_first, output_bias, gain_second, shift_second, shrink_bias, expand_bias, project_bias)
    pack = jnp.concatenate([jnp.pad(v, ((0, 0), (0, 128 - v.shape[1]))) for v in vectors], axis=0).astype(F32)
    length = jnp.where(s == 0, lengths[0, 0], lengths[1, 0]).astype(F32)
    lens = jnp.broadcast_to(length, (8, 128))
    width = jnp.where(s == 0, widths[0], widths[1])
    mask = ((jnp.arange(D) + D * t) < width).astype(F32)[None]
    cos2, sin2 = rotary()

    def mine_of(rows):
        return jnp.where(s == 0, rows[0, 0], rows[1, 0])

    act, ig, sums, fp, fo, fe, fs = core_call(
        mine_of(window_input), mine_of(cotangent), lens, mask, pack, jnp.asarray(cos2), jnp.asarray(sin2),
        project_weight, output_weight, expand_weight, shrink_weight)
    d_pw = fp[:, :24].astype(F32).reshape(4, 24, 3, HW).transpose(1, 2, 0, 3).reshape(1, 24, 3 * D)
    d_ow = fo[:, :24].astype(F32).transpose(1, 0, 2).reshape(1, 24, D)
    d_ew = fe[:, :24].astype(F32).transpose(1, 0, 2).reshape(1, 24, 4 * D)
    d_sw = fs.astype(F32).transpose(1, 0, 2).reshape(1, 96, D)
    totals = jnp.sum(sums[:, :6], axis=0)
    mine = lax.dynamic_slice_in_dim(totals, 24 * chip, 24, axis=1)
    d_eb = lax.dynamic_slice_in_dim(sums[:, 6].reshape(1, 4 * D), 96 * chip, 96, axis=1)
    d_pb = sums[:, 7, :QW].reshape(4, 3, HW).transpose(1, 0, 2).reshape(1, 3 * D)
    d_pb = lax.dynamic_slice_in_dim(d_pb, 72 * chip, 72, axis=1)
    g1, s1, ob, g2, s2, sbias = (mine[i:i + 1] for i in range(6))
    return (act[None, :, None], ig[None, :, None], g1, s1, d_pw, d_pb, d_ow, ob, g2, s2, d_ew, d_eb, d_sw, sbias)


def solution(mesh):
    row = P("section", "dp")
    mat = P("section", "dp", None)
    params = (row, row, mat, row, mat, row, row, row, mat, row, mat, row)
    seq = P(None, "dp", None, None)
    out = P("section", None, "dp", None, None)
    return jax.shard_map(
        per_device, mesh=mesh,
        in_specs=(seq, seq, P(None, "dp"), P()) + params,
        out_specs=(out, out) + params,
        check_vma=False,
    )
```

time: 1940 us -> 358 us (0.18)
  waiting for transfers between devices: 823 us -> 0 us
  blocking collectives: 690 us -> 0 us
  Pallas kernels: 0 us -> 331 us
  matrix products: 242 us -> 0 us
  other arithmetic: 64.8 us -> 4.35 us
  between operations: 32.5 us -> 3.42 us
  loops' own time: 24.1 us -> 0 us
  local copies, waits for them, and re-layouts: 37.5 us -> 17.4 us
    reduce_scatter x4 -> x0, waiting for transfers between devices: 818 us -> none  [the longest x1 277 us: per_device(): lax.psum_scatter(ffn_totals[4], 'dp', scatter_dimension=1, tiled=True)]
    unnamed x2 -> x0, blocking collectives: 690 us -> none
    pallas_call x0 -> x1, Pallas kernels: none -> 331 us  [core_call(): pl.pallas_call(core_kernel, out_shape=[sd((2, T, D), BF), sd((2, T, D), B...]
    dot_general x49 -> x0, matrix products: 242 us -> none  [the longest x3 30.1 us: attention_backward(): jnp.einsum('te,de->td', grad_joined, weights[2], preferred_element_type=j...]
    reduce_sum x36 -> x1, other arithmetic: 29.1 us -> 0.01 us  [per_device(): totals = jnp.sum(sums[:, :6], axis=0)]
    another operation x6 -> x0, loops' own time: 24.1 us -> none  [the longest x3 23.4 us: ffn_backward(): lax.switch(width_level(prefix_width, full_width), branches, normed_second...]
    unnamed x414 -> x14, local copies, waits for them, and re-layouts: 22.5 us -> 1.52 us
  transfers between devices with their start and end apart: 13 -> 0, of which waited for: 6 -> 0; matrix products, arithmetic and copies ran while one was open for 7% -> 0% of each run, Pallas kernels for 0% -> 0%
where the time goes in v1:
time: 358 us; the launch traced here: 357 us
  Pallas kernels  331 us (92%)
  local copies, waits for them, and re-layouts  17.4 us (5%)
  other arithmetic  4.35 us (1%)
    pallas_call x1, Pallas kernels, core_call(): pl.pallas_call(core_kernel, out_shape=[sd((2, T, D), BF), sd((2, T, D), B...  331 us

profile of v1, /device:TPU:32, one launch (start us, length us, event | category | flops | bytes accessed | tf_op | source)
XLA Modules:
  0.0 356.5 jit_solution(9331535375646559965)
XLA Ops:
  0.7 1.3 fusion.1
  3.3 0.6 compare_convert_fusion.mask_ref
  3.9 1.3 fusion.2
  6.5 0.6 broadcast_in_dim.10.len_ref
  7.1 2.0 select_bitcast_fusion
  9.1 0.7 pad.27
  9.8 0.7 pad.28
  10.4 0.7 pad.29
  11.1 0.7 pad.30
  11.7 0.7 pad.31
  12.4 0.7 pad.32
  13.1 0.7 pad.33
  13.7 0.7 pad.34
  14.4 0.6 convert_element_type.33.pack_ref
  15.0 331.3 %shard_map.281 = (bf16[2,64,1536]{2,1,0:T(8,128)(2,1)}, bf16[2,64,1536]{2,1,0:T(8,128)(2,1)}, f32[4,8,1536]{2,1,0:T(8,128)}, bf16[4,32,1152]{2,1,0:T(8,128)(2,1)...) custom-call(bf16[64,1536]{1,0:T(8,128)(2,1)} %get-tuple-element.81.h, ...), custom_call_target="tpu_custom_call" | custom-call | tf_op jit(solution)/shard_map/pallas_call | solution.py:864
  346.3 0.0 copy-start.4
  346.3 0.0 copy-start.2
  346.3 1.0 slice_convert_fusion
  347.4 0.2 reshape.99
  347.6 0.3 copy.42
  347.9 0.0 copy-start.5
  347.9 0.9 reshape.87
  348.8 0.0 copy-done.4
  348.8 0.0 copy-start.3
  348.9 0.0 copy-start.1
  348.9 0.4 copy.45
  349.3 0.0 copy-start
  349.3 1.2 reshape.91
  350.5 0.0 copy-done.2
  350.6 0.5 copy.46
  351.0 1.3 reshape.93
  352.3 0.0 copy-done.5
  352.4 0.7 reshape.89
  353.1 0.0 copy-done.3
  353.1 0.1 constant_dynamic-slice_fusion.2
  353.2 0.5 fusion
  353.8 0.6 constant_dynamic-slice_fusion.1
  354.4 0.6 constant_dynamic-slice_fusion
  355.0 0.0 copy-done.1
  355.0 0.7 copy.51
  355.8 0.0 copy-done
  355.8 0.7 copy.52
  (10 shorter events, 0.3 us)
Async XLA Ops:
  346.3 2.5 copy-start.4
  346.3 4.2 %copy-start.2 = (bf16[2,96,768]{2,1,0:T(8,128)(2,1)S(1)}, bf16[2,96,768]{2,1,0:T(8,128)(2,1)}, u32[]{:S(2)}) copy-start(bf16[2,96,768]{2,1,0:T(8,128)(2,1)} %get-tuple-element.27) | copy-start | bytes 884740
  347.9 4.4 %copy-start.5 = (bf16[4,32,384]{2,1,0:T(8,128)(2,1)S(1)}, bf16[4,32,384]{2,1,0:T(8,128)(2,1)}, u32[]{:S(2)}) copy-start(bf16[4,32,384]{2,1,0:T(8,128)(2,1)} %get-tuple-element.25) | copy-start | bytes 294916
  348.8 4.3 %copy-start.3 = (f32[4,8,1536]{2,1,0:T(8,128)S(1)}, f32[4,8,1536]{2,1,0:T(8,128)}, u32[]{:S(2)}) copy-start(f32[4,8,1536]{2,1,0:T(8,128)} %get-tuple-element.23) | copy-start | bytes 589828
  348.9 6.1 %copy-start.1 = (bf16[2,64,1536]{2,1,0:T(8,128)(2,1)S(1)}, bf16[2,64,1536]{2,1,0:T(8,128)(2,1)}, u32[]{:S(2)}) copy-start(bf16[2,64,1536]{2,1,0:T(8,128)(2,1)} %get-tuple-element.21) | copy-start | bytes 1179652
  349.3 6.5 %copy-start = (bf16[2,64,1536]{2,1,0:T(8,128)(2,1)S(1)}, bf16[2,64,1536]{2,1,0:T(8,128)(2,1)}, u32[]{:S(2)}) copy-start(bf16[2,64,1536]{2,1,0:T(8,128)(2,1)} %get-tuple-element.22) | copy-start | bytes 1179652

commit v2 on v1

v2 whole, which is shorter than its diff:
```python
import jax
import jax.numpy as jnp
import numpy as np
from jax import lax
from jax.experimental import pallas as pl
from jax.experimental.pallas import tpu as pltpu
from jax.sharding import PartitionSpec as P

MESH = pl.DeviceIdType.MESH
ANY = pl.BlockSpec(memory_space=pl.ANY)
VM = pl.BlockSpec(memory_space=pltpu.VMEM)
EPS = 1e-05
MASKED = -1e9
BF = jnp.bfloat16
F32 = jnp.float32
D = 1536
T = 64
TG = 256
HW = 384
QW = 1152
SCALE = 128 ** -0.5
GC = (2 / np.pi) ** 0.5
PR, OU, EX, SH = range(4)
FULL = ((D, QW), (HW, D), (D, D), (D, D))
SLAB = ((48, QW), (48, HW), (48, D), (96, 768))


def nn(a, b):
    return jnp.dot(a, b, preferred_element_type=F32)


def nt(a, b):
    return lax.dot_general(a, b, (((1,), (1,)), ((), ())), preferred_element_type=F32)


def tn(a, b):
    return lax.dot_general(a, b, (((0,), (0,)), ((), ())), preferred_element_type=F32)


def tiles(count, body):
    def step(i, carry):
        body(i)
        return carry
    with jax.named_scope(body.__name__):
        lax.fori_loop(0, count, step, 0)


def span(i, size):
    return pl.ds(pl.multiple_of(i * size, size), size)


def at(start, size, unit):
    return pl.ds(pl.multiple_of(start, unit), size)


def stats(x):
    mean = jnp.mean(x, axis=-1, keepdims=True)
    c = x - mean
    var = jnp.mean(c * c, axis=-1, keepdims=True)
    rs = lax.rsqrt(var + EPS)
    return c * rs, rs


def named(name):
    def deco(fn):
        def inner(*args):
            with jax.named_scope(name):
                return fn(*args)
        return inner
    return deco


def colsum(v):
    return jnp.sum(v, axis=0, keepdims=True)


def to32(v):
    v = v.astype(F32)
    return jnp.concatenate([v, jnp.zeros((8, v.shape[1]), F32)], axis=0).astype(BF)


def core_kernel(win_ref, cot_ref, len_ref, wid_ref, v0, v1, v2, v3, v4, v5, v6, v7, cos_ref, sin_ref, pw, ow, ew, sw,
                act_out, ig_out, sm_out, fp, fo, fe, fs,
                wp, wo, we, ws, r0p, r0o, r0e, r0s, r1p, r1o, r1e, r1s, r2p, r2o, r2e, r2s,
                vp, vo, ve, vs, up, uo, ue, us_,
                normed, ns, gall, dball, qkv, probs, mixed, gder, active, xh1, xh2, rd1, rd2,
                pf, sb, rb, dup, dj, dmix, vis, lens, keep, ostage,
                sp, so, se, cp, co, ce, cs, bp, bo, be, fss,
                tmp, tmp1, allp, small, smt, sme,
                y_s, y_r, w_sem, x_s, x_r, l_s, l_r, z_s, zo_s, z_r, zs_r, p_s, p_r,
                a_s, a_r, b_s, b_r, c_s, c_r, o_sem, q0_s, q0_r, q1_s, q1_r, q2_s, q2_r, t_sem,
                f_s, f_r, e_s, e_r, m_s, m_r, token, f2_r, qf_r, v_sem):
    s = lax.axis_index("section")
    chip = lax.axis_index("dp")
    y, x, z = chip // 16, (chip // 4) % 4, chip % 4
    t = y
    zp = z % 2
    zh = z // 2
    first = s == 0

    def dev(core, cy, cx, cz):
        return (core, cy * 16 + cx * 4 + cz)

    def ypeer(d):
        return dev(s, (y + d) % 4, x, z)

    a_me = jnp.where(first, x, z)
    b_me = jnp.where(first, z, x)

    def grid(a, b):
        return jnp.where(first, a, b), jnp.where(first, b, a)

    def apeer(d):
        cx, cz = grid((a_me + d) % 4, b_me)
        return dev(s, y, cx, cz)

    def bpeer(d):
        cx, cz = grid(a_me, (b_me + d) % 4)
        return dev(s, y, cx, cz)

    sib = dev(1 - s, y, x, z)
    own = at(t * T, T, T)

    bar = pltpu.get_barrier_semaphore()

    def greet(who):
        pl.semaphore_signal(bar, inc=1, device_id=who, device_id_type=MESH)

    with jax.named_scope("greet"):
        for d in (1, 2, 3):
            for core in (s, 1 - s):
                greet(dev(core, (y + d) % 4, x, z))
        for d in (0, 1, 2, 3):
            for core in (s, 1 - s):
                greet(dev(core, (y + d) % 4, x, 2 * zh + 1 - zp))
        greet(sib)
        for d in (1, 2, 3):
            greet(dev(s, y, (x + d) % 4, z))
        for d in (0, 1):
            greet(dev(s, y, x, 2 * (1 - zh) + d))

    def remote(src, dst, ssem, rsem, who):
        return pltpu.make_async_remote_copy(src_ref=src, dst_ref=dst, send_sem=ssem, recv_sem=rsem,
                                            device_id=who, device_id_type=MESH)

    def wait_for(ref, sem):
        pltpu.make_async_copy(ref, ref, sem).wait()

    w_hbm = (wp, wo, we, ws)
    w_v = (vp, vo, ve, vs)
    g_v = (up, uo, ue, us_)
    r0 = (r0p, r0o, r0e, r0s)
    r1 = (r1p, r1o, r1e, r1s)
    r2 = (r2p, r2o, r2e, r2s)

    def slab_at(k, j, cx, cz):
        if k in (PR, EX):
            return at(48 * (8 * (2 * (cz % 2) + j) + 2 * cx + cz // 2), 48, 48), slice(None)
        if k == OU:
            return at(48 * (2 * cx + cz // 2), 48, 48), at(HW * (2 * (cz % 2) + j), HW, HW)
        return at(96 * (4 * cx + cz), 96, 96), at(768 * j, 768, 768)

    def slab_of(ref, k, a, b):
        cx, cz = grid(a, b)
        return ref.at[slab_at(k, s, cx, cz)]

    def parts_of(ref, k, j):
        if k in (PR, EX):
            return [ref.at[at(HW * (2 * p + j), HW, HW)] for p in (0, 1)]
        if k == OU:
            return [ref.at[:, at(HW * (2 * p + j), HW, HW)] for p in (0, 1)]
        return [ref.at[:, at(768 * j, 768, 768)]]

    def bulk(ref, k, slabs):
        if k in (PR, EX):
            return ref.at[pl.ds(0, 48 * slabs)]
        if k == OU:
            return ref.at[pl.ds(0, 12 * slabs)] if slabs > 3 else ref.at[pl.ds(0, 144), pl.ds(0, HW)]
        return ref.at[pl.ds(0, 48 * slabs)]

    def piece_target(yt):
        return dev(y % 2, yt, x, 2 * zh + y // 2), (yt == y) & (s == y % 2) & (zp == y // 2)

    def out_target(q):
        return dev(q % 2, y, x, 2 * zh + q // 2), (zp == q // 2) & (s == q % 2)

    def send_or_keep(src, dst, ssem, rsem, who, is_me):
        @pl.when(is_me)
        def _():
            pltpu.make_async_copy(src, dst, rsem).start()

        @pl.when(jnp.logical_not(is_me))
        def _():
            remote(src, dst, ssem, rsem, who).start()

    def sent(src, dst, ssem, rsem, who, is_me):
        @pl.when(jnp.logical_not(is_me))
        def _():
            remote(src, dst, ssem, rsem, who).wait_send()

    def shard_moves():
        out = []
        for yt in range(4):
            who, me = piece_target(yt)
            out.append((sp.at[yt], cp.at[s, zp], z_s.at[0, yt], z_r.at[0, s, zp], who, me))
        for q in range(4):
            who, me = out_target(q)
            out.append((so.at[q], co.at[s, zp], z_s.at[1, q], z_r.at[1, s, zp], who, me))
        for yt in range(4):
            who, me = piece_target(yt)
            out.append((se.at[yt], ce.at[s, zp], z_s.at[2, yt], z_r.at[2, s, zp], who, me))
        for j in range(2):
            out.append((sw.at[0, :, pl.ds(768 * j, 768)], cs.at[s], zo_s.at[j], zs_r.at[s],
                        dev(j, y, x, z), s == j))
        return out

    moves = shard_moves()
    with jax.named_scope("shards"):
        for yt in range(4):
            sp[yt] = to32(jnp.concatenate([pw[0, :, p * D + HW * yt:p * D + HW * (yt + 1)] for p in range(3)], axis=1))
        for q in range(4):
            so[q] = to32(ow[0, :, HW * q:HW * (q + 1)])
        for yt in range(4):
            se[yt] = to32(ew[0, :, D * yt:D * (yt + 1)])

    allp[s, pl.ds(chip, 1)] = jnp.zeros((1, 8, 128), F32)
    for r, v in enumerate((v0, v1, v2, v3, v4, v5, v6, v7)):
        allp[s, pl.ds(chip, 1), r:r + 1, 0:v.shape[1]] = v[...].astype(F32)[None]

    def pack_copies(stage):
        out = []
        for d in (1, 2, 3):
            if stage == 0:
                blk, who = allp.at[s, pl.ds(chip, 1)], dev(s, y, x, (z + d) % 4)
            elif stage == 1:
                blk, who = allp.at[s, at(chip - z, 4, 4)], dev(s, y, (x + d) % 4, z)
            else:
                blk, who = allp.at[s, at(16 * y, 16, 16)], ypeer(d)
            out.append(remote(blk, blk, p_s.at[stage, d - 1], p_r.at[stage, d - 1], who))
        return out

    @named("pack go")
    def pack_go(stage):
        for c in pack_copies(stage):
            c.start()

    @named("pack wait")
    def pack_end(stage):
        for c in pack_copies(stage):
            c.wait()

    length = len_ref[s, 0].astype(F32)
    width = wid_ref[s]
    lens[pl.ds(t, 1)] = jnp.full((1, 8, 128), length, F32)
    lcs = [remote(lens.at[pl.ds(t, 1)], lens.at[pl.ds(t, 1)], l_s.at[d - 1], l_r.at[d - 1], ypeer(d)) for d in (1, 2, 3)]

    got = (cp, co, ce, cs)
    bld = (bp, bo, be, cs)

    def home(l, k):
        return w_hbm[k].at[1] if l else w_v[k]

    def a_copies(l, k):
        src = bld[k].at[l]
        return [remote(src, slab_of(home(l, k), k, a_me, b_me), a_s.at[l, k], a_r.at[l, k], apeer(d))
                for d in (1, 2, 3)]

    def own_copy(l, k):
        return pltpu.make_async_copy(bld[k].at[l], slab_of(home(l, k), k, a_me, b_me), o_sem.at[l, k])

    @named("gather a")
    def gather_a(l, k):
        if k == SH:
            wait_for(cs.at[l], zs_r.at[l])
        else:
            zk = (0, 1, 2)[k]
            for p in (0, 1):
                wait_for(got[k].at[l, p], z_r.at[zk, l, p])
            halves = [got[k][l, p].astype(F32)[:24] for p in (0, 1)]
            bld[k][l] = jnp.concatenate(halves, axis=0).astype(BF)
        for c in a_copies(l, k):
            c.start()
        own_copy(l, k).start()

    @named("gather b")
    def gather_b(l, k):
        w = home(l, k)
        wait_for(bulk(w, k, 3), a_r.at[l, k])
        own_copy(l, k).wait()
        for a in range(4):
            src = slab_of(w, k, a, b_me)
            for side, d in ((0, 1), (1, 3)):
                remote(src, src, b_s.at[l, k], b_r.at[side, l, k], bpeer(d)).start()

    @named("gather f")
    def gather_f(l, k):
        w = home(l, k)
        for side, d in ((0, 1), (1, 3)):
            wait_for(bulk(w, k, 4), b_r.at[side, l, k])
            for a in (2 * side, 2 * side + 1):
                src = slab_of(w, k, a, (b_me + 4 - d) % 4)
                remote(src, src, b_s.at[l, k], f2_r.at[l, k], bpeer(d)).start()

    @named("gather c")
    def gather_c(l, k):
        w = home(l, k)
        wait_for(bulk(w, k, 4), f2_r.at[l, k])
        for blk in parts_of(w, k, s):
            remote(blk, blk, c_s.at[l, k], c_r.at[l, k], sib).start()

    @named("gather d")
    def gather_d(l, k):
        wait_for(bulk(home(l, k), k, 16), c_r.at[l, k])
        if l == 0:
            save(k).start()

    def save(k):
        return pltpu.make_async_copy(w_v[k], w_hbm[k].at[0], v_sem.at[k])

    @named("gather drain")
    def gather_drain(l, k):
        w = home(l, k)
        wait_for(bulk(w, k, 3), a_s.at[l, k])
        wait_for(bulk(w, k, 12), b_s.at[l, k])
        wait_for(bulk(w, k, 16), c_s.at[l, k])

    def gbuf(l, k):
        if l == 0 and k == PR:
            return us_.at[:, pl.ds(0, QW)]
        return g_v[k] if l else w_v[k]

    @named("sum0 go")
    def sum0_go(l, k):
        for i, blk in enumerate(parts_of(gbuf(l, k), k, 1 - s)):
            dst = r0[k].at[l, i] if k != SH else r0[k].at[l]
            remote(blk, dst, q0_s.at[l, k], q0_r.at[l, k], sib).start()

    def halves_tmp(k):
        if k in (PR, EX):
            return [tmp.at[pl.ds(HW * p, HW), pl.ds(0, FULL[k][1])] for p in (0, 1)]
        if k == OU:
            return [tmp.at[pl.ds(HW * p, HW), pl.ds(0, HW)] for p in (0, 1)]
        return [tmp.at[:, pl.ds(768 * p, 768)] for p in (0, 1)]

    def sum0_copies(l, k):
        srcs = [r0[k].at[l, i] for i in (0, 1)] if k != SH else [r0[k].at[l, pl.ds(768 * i, 768)] for i in (0, 1)]
        return [pltpu.make_async_copy(a, b, t_sem.at[i]) for i, (a, b) in enumerate(zip(srcs, halves_tmp(k)))]

    @named("sum0 load")
    def sum0_load(l, k):
        wait_for(r0[k].at[l], q0_r.at[l, k])
        for c in sum0_copies(l, k):
            c.start()

    @named("sum0")
    def sum0_fin(l, k):
        g = gbuf(l, k)
        cps = sum0_copies(l, k)
        for p in (0, 1):
            cps[p].wait()

            def add(i):
                if k in (PR, EX):
                    rows, cols, n = at(HW * (2 * p + s) + 96 * i, 96, 96), slice(None), FULL[k][1]
                    other = tmp[pl.ds(pl.multiple_of(HW * p + 96 * i, 96), 96), 0:n]
                elif k == OU:
                    rows, cols = span(i, 96), at(HW * (2 * p + s), HW, HW)
                    other = tmp[pl.ds(pl.multiple_of(HW * p + 96 * i, 96), 96), 0:HW]
                else:
                    rows, cols = at(768 * p + 96 * i, 96, 96), at(768 * s, 768, 768)
                    other = tmp[span(i, 96), 768 * p:768 * p + 768]
                g[rows, cols] = (g[rows, cols].astype(F32) + other.astype(F32)).astype(BF)
            tiles(8 if k == SH else 4, add)
        for a in (0, 2, 1, 3):
            far = 1 if a < 2 else 3
            remote(slab_of(g, k, a, (b_me + 2) % 4), r1_slab(l, k, 0, a), q1_s.at[l, k], qf_r.at[l, k], bpeer(far)).start()
        for a in (0, 2, 1, 3):
            near = 3 if a < 2 else 1
            remote(slab_of(g, k, a, (b_me + near) % 4), r1_slab(l, k, near, a), q1_s.at[l, k], q1_r.at[l, k],
                   bpeer(near)).start()

    def r1_slab(l, k, d, a):
        rows = SLAB[k][0]
        return r1[k].at[l, (0, 1, None, 2)[d], pl.ds(rows * a, rows)]

    def tmp_set(k, side):
        rows, cols = SLAB[k]
        if k == SH:
            return tmp1.at[pl.ds(0, 4 * rows), pl.ds(cols * side, cols)]
        return tmp1.at[pl.ds(4 * rows * side, 4 * rows), pl.ds(0, cols)]

    def tmp_slab(k, side, a):
        rows, cols = SLAB[k]
        if k == SH:
            return tmp1[at(rows * a, rows, rows), cols * side:cols * (side + 1)].astype(F32)
        return tmp1[at(4 * rows * side + rows * a, rows, rows), 0:cols].astype(F32)

    @named("sum1 pass on")
    def sum1_mid(l, k):
        g = gbuf(l, k)
        wait_for(r1[k].at[l, 0], qf_r.at[l, k])
        c = pltpu.make_async_copy(r1[k].at[l, 0], tmp_set(k, 0), t_sem.at[2])
        c.start()
        c.wait()
        for a in range(4):
            d = 1 if a < 2 else 3
            cx, cz = grid(a, (b_me + d) % 4)
            where = slab_at(k, s, cx, cz)
            g[where] = (g[where].astype(F32) + tmp_slab(k, 0, a)).astype(BF)
            remote(g.at[where], r1_slab(l, k, d, a), q1_s.at[l, k], q1_r.at[l, k], bpeer(d)).start()

    @named("sum1")
    def sum1_end(l, k):
        g = gbuf(l, k)
        wait_for(r1[k].at[l, pl.ds(1, 2)], q1_r.at[l, k])
        cps = [pltpu.make_async_copy(r1[k].at[l, 1 + i], tmp_set(k, i), t_sem.at[3 + i]) for i in (0, 1)]
        go(cps)
        end(cps)
        for da in (2, 1, 3, 0):
            a = (a_me + da) % 4
            cx, cz = grid(a, b_me)
            where = slab_at(k, s, cx, cz)
            total = g[where].astype(F32) + tmp_slab(k, 0, a) + tmp_slab(k, 1, a)
            if da == 0:
                bld[k][l] = total.astype(BF)
            else:
                g[where] = total.astype(BF)
                remote(g.at[where], r2[k].at[l, da - 1], q2_s.at[l, k], q2_r.at[l, k], apeer(da)).start()

    fsend = (sp, so, se, fss)
    frecv = (fp, fo, fe, fs)

    def last_moves(l, k):
        out = []
        if k == SH:
            out.append((fss.at[l], fs.at[s], f_s.at[l, k, 0], f_r.at[k, s], dev(l, y, x, z), s == l))
            return out
        for p in (0, 1):
            if k == OU:
                q = 2 * zp + s
                who, me, slot = dev(l, y, x, 2 * zh + p), (s == l) & (zp == p), q
            else:
                yo = 2 * zp + s
                who, me, slot = dev(l, yo, x, 2 * zh + p), (s == l) & (yo == y) & (zp == p), y
            out.append((fsend[k].at[2 * l + p], frecv[k].at[slot], f_s.at[l, k, p], f_r.at[k, slot], who, me))
        return out

    @named("sum2")
    def sum2_end(l, k):
        wait_for(r2[k].at[l], q2_r.at[l, k])
        rows, cols = SLAB[k]
        spots = [tmp1.at[pl.ds(rows * d, rows), pl.ds(0, cols)] for d in range(3)]
        cps = [pltpu.make_async_copy(r2[k].at[l, d], spots[d], t_sem.at[5 + d]) for d in range(3)]
        go(cps)
        end(cps)
        total = bld[k][l].astype(F32)
        for d in range(3):
            total = total + tmp1[rows * d:rows * (d + 1), 0:cols].astype(F32)
        if k == SH:
            fss[l] = total.astype(BF)
        else:
            for p in (0, 1):
                fsend[k][2 * l + p] = to32(total[24 * p:24 * (p + 1)])
        for m in last_moves(l, k):
            send_or_keep(*m)

    @named("sum drain")
    def sum_drain(l, k):
        wait_for(r0[k].at[l], q0_s.at[l, k])
        wait_for(r1[k].at[l], q1_s.at[l, k])
        wait_for(r2[k].at[l], q2_s.at[l, k])

    @named("last weights")
    def finish_weights():
        for l in (0, 1):
            for k in range(4):
                for m in last_moves(l, k):
                    sent(*m)
        for k in range(4):
            for i in range(2 if k == SH else 4):
                wait_for(frecv[k].at[i], f_r.at[k, i])

    def vec_copies(stage):
        out = []
        if stage == 0:
            out.append(remote(smt.at[1 - s], sme.at[0, 0], e_s.at[0, 0], e_r.at[0, 0], sib))
            return out
        for d in (1, 2, 3):
            if stage == 1:
                who = apeer(d)
            elif stage == 2:
                who = bpeer(d)
            else:
                out.append(remote(sm_out.at[t], sm_out.at[t], e_s.at[3, d - 1], e_r.at[3, d - 1], ypeer(d)))
                continue
            out.append(remote(smt.at[2 + stage], sme.at[stage, d - 1], e_s.at[stage, d - 1], e_r.at[stage, d - 1], who))
        return out

    @named("vectors go")
    def vec_go(stage):
        for c in vec_copies(stage):
            c.start()

    @named("vectors wait")
    def vec_end(stage):
        for c in vec_copies(stage):
            c.wait()
        if stage == 0:
            smt[3] = smt[pl.ds(s, 1)][0] + sme[0, 0]
        elif stage == 1:
            smt[4] = smt[3] + sme[1, 0] + sme[1, 1] + sme[1, 2]
        elif stage == 2:
            sm_out[pl.ds(t, 1)] = (smt[4] + sme[2, 0] + sme[2, 1] + sme[2, 2])[None]

    def wcopy(k, l):
        return pltpu.make_async_copy(w_hbm[k].at[l], w_v[k], w_sem.at[k])

    LEFT, RIGHT = slice(0, 768), slice(768, D)
    COLS = (pl.ds(0, 768), pl.ds(768, 768))
    right, left = ypeer(1), ypeer(3)

    def rows_of(d):
        return at((t + d) % 4 * T, T, T)

    def ysent(buf, i):
        for side in (0, 1):
            wait_for(buf.at[pl.ds(0, 96)], y_s.at[i, side])

    def ag_go(buf, idx):
        for c, side, slot in ((0, 0, 0), (1, 1, 1), (1, 0, 2), (0, 1, 3)):
            blk = buf.at[own, COLS[c]]
            remote(blk, blk, y_s.at[idx, side], y_r.at[idx, slot], (right, left)[side]).start()

    @named("y pass on")
    def ag_pass(buf, idx):
        for side, d in ((0, 3), (1, 1)):
            wait_for(buf.at[pl.ds(0, T), COLS[side]], y_r.at[idx, side])
            blk = buf.at[rows_of(d), COLS[side]]
            remote(blk, blk, y_s.at[idx, side], y_r.at[idx, 2 + side], (right, left)[side]).start()

    @named("y wait")
    def ag_end(buf, idx):
        for slot in (2, 3):
            wait_for(buf.at[pl.ds(0, T)], y_r.at[idx, slot])
        ysent(buf, idx)

    def go(cps):
        for c in cps:
            c.start()

    @named("y wait")
    def end(cps):
        for c in cps:
            c.wait()

    def reduce_go(idx, name, product):
        def tile(i):
            c = span(i, 768)
            pf[:, c] = product(c)
            sb[0, :, c] = pf[rows_of(2), c].astype(BF)
            remote(sb.at[0, :, c], rb.at[idx % 2, 2, :, c], y_s.at[8 + idx, i], y_r.at[8 + idx, i], ypeer(1 + 2 * i)).start()
            sb[1, :, c] = pf[rows_of(3 - 2 * i), c].astype(BF)
            remote(sb.at[1, :, c], rb.at[idx % 2, 1 - i, :, c], y_s.at[8 + idx, 1 - i], y_r.at[8 + idx, 3 - i],
                   ypeer(3 - 2 * i)).start()
        tile.__name__ = name
        tiles(2, tile)

    @named("y pass on")
    def reduce_pass(idx):
        for side, d in ((0, 1), (1, 3)):
            c = (LEFT, RIGHT)[side]
            wait_for(rb.at[idx % 2, 2, :, COLS[side]], y_r.at[8 + idx, side])
            sb[2, :, c] = (pf[rows_of(d), c] + rb[idx % 2, 2, :, c].astype(F32)).astype(BF)
            remote(sb.at[2, :, COLS[side]], rb.at[idx % 2, side, :, COLS[side]], y_s.at[8 + idx, side],
                   y_r.at[8 + idx, 2 + side], (right, left)[side]).start()

    @named("y wait")
    def reduce_end(idx):
        for side in (0, 1):
            wait_for(rb.at[idx % 2, side], y_r.at[8 + idx, 2 + side])
        ysent(gall, 8 + idx)
        return pf[own, :] + rb[idx % 2, 0].astype(F32) + rb[idx % 2, 1].astype(F32)

    livef = jnp.where(lax.broadcasted_iota(jnp.int32, (T, D), 0).astype(F32) < length, 1.0, 0.0)

    def put_result(l, ref, value, way):
        @pl.when(s == l)
        def _():
            ref[pl.ds(s, 1)] = value[None]

        @pl.when(s != l)
        def _():
            ostage[way] = value
            remote(ostage.at[way], ref.at[s], x_s.at[way], x_r.at[way], sib).start()

    @named("last results")
    def finish_results():
        for way, ref in enumerate((act_out, ig_out)):
            remote(ostage.at[way], ref.at[s], x_s.at[way], x_r.at[way], sib).wait()

    def nothing():
        pass

    def forward(l, hidden, hooks):
        hook = lambda name: hooks.get(name, nothing)()
        if l:
            with jax.named_scope("norm first"):
                xh, rsd = stats(hidden)
                xh1[l] = xh
                rd1[l] = jnp.broadcast_to(rsd, (T, 128))
                normed[l, own, :] = (xh * small[l, 0:1, :] + small[l, 1:2, :]).astype(BF)
            ag_go(normed.at[l], l * 2)
            hook("normed")
            ag_pass(normed.at[l], l * 2)
            hook("normed2")
            ag_end(normed.at[l], l * 2)
        if l:
            wcopy(PR, 1).wait()
        with jax.named_scope("queries keys values"):
            for part in range(3):
                joined = nn(normed[l], vp[:, part * HW:(part + 1) * HW]) + small[l, 7:8, part * HW:(part + 1) * HW]
                for h in range(3):
                    v = joined[:, h * 128:(h + 1) * 128]
                    if part < 2:
                        v = v * cos_ref[...] + pltpu.roll(v, 64, 1) * sin_ref[...]
                    qkv[l, :, part * HW + h * 128:part * HW + (h + 1) * 128] = v.astype(BF)
        hook("joined")
        with jax.named_scope("attention"):
            for h in range(3):
                q = qkv[l, :, h * 128:(h + 1) * 128]
                k = qkv[l, :, HW + h * 128:HW + (h + 1) * 128]
                v = qkv[l, :, 2 * HW + h * 128:2 * HW + (h + 1) * 128]
                sc = jnp.where(vis[...] > 0.5, nt(q, k) * SCALE, MASKED)
                top = jnp.max(sc, axis=-1, keepdims=True)
                ex = jnp.exp(sc - top)
                p = ex * (1.0 / jnp.sum(ex, axis=-1, keepdims=True))
                probs[l, h] = p
                mixed[l, :, h * 128:(h + 1) * 128] = nn(p.astype(BF), v).astype(BF)
        if l:
            wcopy(OU, 1).wait()
        reduce_go(l * 2, "out_tile", lambda c: nn(mixed[l], vo[:, c]))
        hook("mixed")
        reduce_pass(l * 2)
        hook("mixed2")
        middle = hidden + reduce_end(l * 2) + small[l, 2:3, :]
        with jax.named_scope("norm second"):
            xh, rsd = stats(middle)
            xh2[l] = xh
            rd2[l] = jnp.broadcast_to(rsd, (T, 128))
            ns[l, own, :] = (xh * small[l, 3:4, :] + small[l, 4:5, :]).astype(BF)
            keep[...] = middle
        ag_go(ns.at[l], l * 2 + 1)
        hook("second")
        ag_pass(ns.at[l], l * 2 + 1)
        hook("second2")
        ag_end(ns.at[l], l * 2 + 1)
        if l:
            wcopy(EX, 1).wait()

        def up_tile(i):
            c = span(i, 256)
            u = nn(ns[l], ve[:, c]) + small[l, 6:7, c]
            unit = lax.broadcasted_iota(jnp.int32, (1, 256), 1) + (i * 256 + D * t)
            m = jnp.where(unit < width, 1.0, 0.0)
            u2 = u * u
            th = jnp.tanh(GC * u * (1.0 + 0.044715 * u2))
            half = 0.5 * (1.0 + th)
            active[l, :, c] = (u * half * m).astype(BF)
            gder[l, :, c] = m * (half + 0.5 * u * (1.0 - th * th) * (GC * (1.0 + 3 * 0.044715 * u2)))
        tiles(6, up_tile)
        hook("upper")
        if l:
            wcopy(SH, 1).wait()
        reduce_go(l * 2 + 1, "down_tile", lambda c: nn(active[l], vs[:, c]))
        if l == 0:
            hook("down")
            reduce_pass(1)
            hook("down2")
            return out_rows(0)

    def out_rows(l):
        result = (keep[...] + reduce_end(l * 2 + 1) + small[l, 5:6, :]) * livef
        result = result.astype(BF)
        put_result(l, act_out, result, 0)
        return result

    def norm_back(dn, xh, rsd, gain):
        e = dn * gain
        return rsd[:, 0:1] * (e - jnp.mean(e, axis=-1, keepdims=True)
                              - xh * jnp.mean(e * xh, axis=-1, keepdims=True))

    def backward(l, g, hooks):
        hook = lambda name: hooks.get(name, nothing)()
        g32 = g.astype(F32)
        smt[l, 5:6, :] = colsum(g32)
        if l == 0:
            gall[own, :] = g
        if l == 0:
            ag_go(gall, 4)
            hook("grad")
            ag_pass(gall, 4)
            hook("grad2")
            ag_end(gall, 4)

        def gs_tile(i):
            c = span(i, 256)
            gbuf(l, SH)[c, :] = tn(active[l, :, c], gall[...]).astype(BF)

        def dact_tile(i):
            c = span(i, 256)
            da = nt(gall[...], vs[c, :]) * gder[l, :, c]
            da = da.astype(BF)
            dup[:, c] = da
            smt[l, 6:7, c] = colsum(da.astype(F32))

        def ge_tile(i):
            c = span(i, 256)
            gbuf(l, EX)[c, :] = tn(ns[l, :, c], dup[...]).astype(BF)

        if l == 0:
            wcopy(SH, 0).wait()
            tiles(6, dact_tile)
            wcopy(EX, 0).wait()
        else:
            end(g_cps)
            tiles(6, gs_tile)
            sum0_go(1, SH)
            tiles(6, dact_tile)
            wcopy(SH, 0).start()
            hook("result")
            reduce_pass(3)
            hook("result2")
            out_rows(1)
        reduce_go(4 + l * 2, "e_tile", lambda c: nt(dup[...], ve[c, :]))
        if l == 1:
            wcopy(EX, 0).start()
        else:
            tiles(6, gs_tile)
            sum0_go(0, SH)
        tiles(6, ge_tile)
        sum0_go(l, EX)
        hook("upper")
        reduce_pass(4 + l * 2)
        hook("upper2")
        dn = reduce_end(4 + l * 2)
        with jax.named_scope("norm second back"):
            smt[l, 3:4, :] = colsum(dn * xh2[l])
            smt[l, 4:5, :] = colsum(dn)
            dmid = g32 + norm_back(dn, xh2[l], rd2[l], small[l, 3:4, :])
            db = dmid.astype(BF)
            smt[l, 2:3, :] = colsum(db.astype(F32))
            keep[...] = dmid
            dball[own, :] = db
        ag_go(dball, 4 + l * 2 + 1)
        hook("middle")
        ag_pass(dball, 4 + l * 2 + 1)
        hook("middle2")
        ag_end(dball, 4 + l * 2 + 1)
        if l == 0:
            wcopy(OU, 0).wait()
        dmix[...] = nt(dball[...], vo[...]).astype(BF)
        if l == 1:
            wcopy(OU, 0).start()
        with jax.named_scope("attention back"):
            for h in range(3):
                c = slice(h * 128, (h + 1) * 128)
                q = qkv[l, :, h * 128:(h + 1) * 128]
                k = qkv[l, :, HW + h * 128:HW + (h + 1) * 128]
                v = qkv[l, :, 2 * HW + h * 128:2 * HW + (h + 1) * 128]
                p = probs[l, h]
                dm = dmix[:, c]
                dj[:, 2 * HW + h * 128:2 * HW + (h + 1) * 128] = tn(p.astype(BF), dm).astype(BF)
                dp = nt(dm, v)
                dsc = (p * (dp - jnp.sum(dp * p, axis=-1, keepdims=True))).astype(BF)
                for part, v in ((0, nn(dsc, k)), (1, tn(dsc, q))):
                    v = v * SCALE
                    v = v * cos_ref[...] - pltpu.roll(v, 64, 1) * sin_ref[...]
                    dj[:, part * HW + h * 128:part * HW + (h + 1) * 128] = v.astype(BF)
        smt[l, 7:8, :] = jnp.zeros((1, D), F32)
        smt[l, 7:8, 0:QW] = colsum(dj[...].astype(F32))
        if l == 0:
            wcopy(PR, 0).wait()

        def gp_tile(i):
            c = span(i, 256)
            gbuf(l, PR)[c, :] = tn(normed[l, :, c], dj[...]).astype(BF)
        tiles(6, gp_tile)
        sum0_go(l, PR)
        reduce_go(4 + l * 2 + 1, "d_tile", lambda c: nt(dj[...], vp[c, :]))
        if l == 1:
            wcopy(PR, 0).start()
        with jax.named_scope("output term"):
            gbuf(l, OU)[...] = tn(mixed[l], dball[...]).astype(BF)
        sum0_go(l, OU)
        hook("joined")
        reduce_pass(4 + l * 2 + 1)
        hook("joined2")
        dn = reduce_end(4 + l * 2 + 1)
        with jax.named_scope("norm first back"):
            smt[l, 0:1, :] = colsum(dn * xh1[l])
            smt[l, 1:2, :] = colsum(dn)
            dh = keep[...] + norm_back(dn, xh1[l], rd1[l], small[l, 0:1, :])
            res = dh.astype(BF)
        put_result(l, ig_out, res, 1)
        return res

    hall = dball
    hall[own, :] = win_ref[s]
    h_cps = [remote(hall.at[own], hall.at[own], m_s.at[d - 1], m_r.at[d - 1], ypeer(d)) for d in (1, 2, 3)]
    g_cps = [remote(gall.at[own], gall.at[own], m_s.at[2 + d], m_r.at[2 + d], ypeer(d)) for d in (1, 2, 3)]
    pack_last = remote(allp.at[s], allp.at[s], p_s.at[3, 0], p_r.at[3, 0], sib)
    with jax.named_scope("greet wait"):
        pl.semaphore_wait(bar, 20)
    pack_go(0)
    go(lcs)

    @pl.when(first)
    def _():
        for m in moves[:4]:
            send_or_keep(*m)
    go(h_cps)
    gather_a(0, PR)

    @pl.when(first)
    def _():
        for m in moves[4:8]:
            send_or_keep(*m)
    for m in moves[12:]:
        send_or_keep(*m)
    pack_end(0)
    pack_go(1)
    gather_b(0, PR)
    gather_a(0, OU)
    pack_end(1)
    pack_go(2)
    end(lcs)
    row = lax.broadcasted_iota(jnp.int32, (TG, TG), 0)
    col = lax.broadcasted_iota(jnp.int32, (TG, TG), 1)
    limit = jnp.zeros((1, TG), F32)
    blk = lax.broadcasted_iota(jnp.int32, (1, TG), 1) // T
    for r in range(4):
        one = lens[r][0:1, :]
        limit = jnp.where(blk == r, jnp.concatenate([one, one], axis=1), limit)
    ok = (row // T == col // T) & (col <= row) & ((col % T).astype(F32) < limit)
    vis[...] = jnp.where(ok, 1.0, 0.0)
    hidden0 = win_ref[s].astype(F32)
    xh, rsd = stats(hidden0)
    xh1[0] = xh
    rd1[0] = jnp.broadcast_to(rsd, (T, 128))
    gall[own, :] = (cot_ref[s].astype(F32) * livef).astype(BF)
    gather_f(0, PR)

    @pl.when(first)
    def _():
        for m in moves[8:12]:
            send_or_keep(*m)
    gather_b(0, OU)
    pack_end(2)
    pack_last.start()
    gather_c(0, PR)
    gather_a(0, EX)
    gather_a(0, SH)
    gather_f(0, OU)
    go(g_cps)
    end(h_cps)
    pack_last.wait()

    def spread(rows, width, total):
        n = lax.broadcasted_iota(jnp.int32, (128, total), 1)
        i = lax.broadcasted_iota(jnp.int32, (128, total), 0)
        pick = jnp.where(n - (n // width) * width == i, 1.0, 0.0).astype(BF)
        wide = nn(rows.astype(BF), pick)
        n = lax.broadcasted_iota(jnp.int32, (64, total), 1)
        c = lax.broadcasted_iota(jnp.int32, (64, total), 0)
        return colsum(jnp.where(n // width == c, wide, 0.0))

    @named("spread")
    def unpack(l, wanted):
        for r in wanted:
            if r < 6:
                small[l, r:r + 1, :] = spread(allp[l, :, r, :], 24, D)
            elif r == 6:
                mine = allp[l, at(16 * t, 16, 16), 6, :]
                n = lax.broadcasted_iota(jnp.int32, (128, D), 1)
                i = lax.broadcasted_iota(jnp.int32, (128, D), 0)
                pick = jnp.where(n - (n // 96) * 96 == i, 1.0, 0.0).astype(BF)
                wide = nn(mine.astype(BF), pick)
                n = lax.broadcasted_iota(jnp.int32, (16, D), 1)
                c = lax.broadcasted_iota(jnp.int32, (16, D), 0)
                small[l, 6:7, :] = colsum(jnp.where(n // 96 == c, wide, 0.0))
            else:
                n = lax.broadcasted_iota(jnp.int32, (128, QW), 1)
                i = lax.broadcasted_iota(jnp.int32, (128, QW), 0)
                n = n + (n // HW) * (D - HW) + HW * t
                pick = jnp.where(n - (n // 72) * 72 == i, 1.0, 0.0).astype(BF)
                wide = nn(allp[l, :, 7, :].astype(BF), pick)
                n = lax.broadcasted_iota(jnp.int32, (64, QW), 1)
                c = lax.broadcasted_iota(jnp.int32, (64, QW), 0)
                n = n + (n // HW) * (D - HW) + HW * t
                small[l, 7:8, 0:QW] = colsum(jnp.where(n // 72 == c, wide, 0.0))

    unpack(0, (0, 1, 7))

    def norm_tile(i):
        rows = span(i, T)
        wide, _ = stats(hall[rows, :].astype(F32))
        normed[0, rows, :] = (wide * small[0, 0:1, :] + small[0, 1:2, :]).astype(BF)
    tiles(4, norm_tile)
    gather_b(0, EX)
    gather_c(0, OU)
    gather_d(0, PR)

    def steps(*todo):
        def run():
            for what, *args in todo:
                what(*args)
        return run

    def second_shards():
        @pl.when(jnp.logical_not(first))
        def _():
            for m in moves[8:12]:
                send_or_keep(*m)

    def reload(k):
        gather_drain(0, k)
        save(k).wait()
        gather_d(1, k)
        wcopy(k, 1).start()

    ga, gb, gf, gc, gd = gather_a, gather_b, gather_f, gather_c, gather_d
    def second_first():
        @pl.when(jnp.logical_not(first))
        def _():
            for m in moves[:8]:
                send_or_keep(*m)

    first_hooks = dict(
        joined=steps((gb, 0, SH), (gd, 0, OU)),
        mixed=steps((second_first,), (unpack, 0, (2, 3, 4, 5, 6))),
        mixed2=steps((gf, 0, EX), (second_shards,), (ga, 1, PR), (ga, 1, OU), (gc, 0, EX)),
        second=steps((gf, 0, SH)),
        second2=steps((gb, 1, PR), (ga, 1, EX), (gc, 0, SH), (gd, 0, EX)),
        upper=steps((gb, 1, OU), (gd, 0, SH)),
        down=steps((unpack, 1, (0, 1, 2, 3, 4, 5, 6, 7)), (ga, 1, SH)),
        down2=steps((gf, 1, PR), (gb, 1, EX), (gf, 1, OU), (gc, 1, PR)))
    second_hooks = dict(
        normed2=steps((gb, 1, SH), (gc, 1, OU), (gf, 1, EX), (reload, PR)),
        joined=steps((reload, OU)),
        mixed2=steps((gc, 1, EX), (gf, 1, SH)),
        second2=steps((gc, 1, SH), (reload, EX)),
        upper=steps((reload, SH)))
    a1 = forward(0, hidden0, first_hooks)
    forward(1, a1.astype(F32), second_hooks)

    for k in range(4):
        gather_drain(1, k)
    for m in moves:
        sent(*m)

    load, fin, mid, last = sum0_load, sum0_fin, sum1_mid, sum1_end
    ig2 = backward(1, gall[own, :], dict(
        result2=steps((load, 1, SH), (fin, 1, SH)),
        upper2=steps((mid, 1, SH), (load, 1, EX), (fin, 1, EX)),
        middle2=steps((last, 1, SH), (mid, 1, EX)),
        joined=steps((load, 1, PR), (fin, 1, PR)),
        joined2=steps((load, 1, OU), (last, 1, EX), (fin, 1, OU))))
    g1 = (ig2.astype(F32) * livef).astype(BF)
    backward(0, g1, dict(
        grad=steps((sum2_end, 1, SH), (sum_drain, 1, SH)),
        grad2=steps((mid, 1, PR), (mid, 1, OU), (sum2_end, 1, EX)),
        upper2=steps((load, 0, SH), (last, 1, PR), (fin, 0, SH)),
        middle=steps((load, 0, EX), (last, 1, OU), (fin, 0, EX)),
        middle2=steps((mid, 0, SH), (sum2_end, 1, PR)),
        joined=steps((load, 0, PR), (fin, 0, PR)),
        joined2=steps((load, 0, OU), (mid, 0, EX), (fin, 0, OU), (last, 0, SH))))
    vec_go(0)
    vec_end(0)
    vec_go(1)
    last(0, EX)
    mid(0, PR)
    mid(0, OU)
    sum2_end(1, OU)
    sum2_end(0, SH)
    vec_end(1)
    vec_go(2)
    last(0, PR)
    last(0, OU)
    sum2_end(0, EX)
    vec_end(2)
    vec_go(3)
    sum2_end(0, PR)
    sum2_end(0, OU)
    vec_end(3)
    finish_weights()
    finish_results()
    for k in range(4):
        for l in (0, 1):
            if (l, k) != (1, SH):
                sum_drain(l, k)


def finish_kernel(act, ig, sums, fp, fo, fe, fs,
                  act_out, ig_out, o0, o1, d_pw, o7, d_ow, o2, o3, o4, d_ew, o6, d_sw, o5):
    chip = lax.axis_index("dp")
    act_out[0, :, 0] = act[...]
    ig_out[0, :, 0] = ig[...]
    for r in range(4):
        for p in range(3):
            d_pw[0, :, p * D + HW * r:p * D + HW * (r + 1)] = fp[r, :, HW * p:HW * (p + 1)].astype(F32)[:24]
        d_ow[0, :, HW * r:HW * (r + 1)] = fo[r].astype(F32)[:24]
        d_ew[0, :, D * r:D * (r + 1)] = fe[r].astype(F32)[:24]
    for j in range(2):
        d_sw[0, :, 768 * j:768 * (j + 1)] = fs[j].astype(F32)
    total = sums[0] + sums[1] + sums[2] + sums[3]
    mine = pltpu.roll(total, (D - 24 * chip) % D, 1)
    for r, o in enumerate((o0, o1, o2, o3, o4, o5)):
        o[...] = mine[r:r + 1, :24]
    units = sums[chip // 16]
    o6[...] = pltpu.roll(units, (D - 96 * (chip % 16)) % D, 1)[6:7, :96]
    cols = jnp.concatenate([sums[r, :, HW * p:HW * (p + 1)] for p in range(3) for r in range(4)], axis=1)
    o7[...] = pltpu.roll(cols, (3 * D - 72 * chip) % (3 * D), 1)[7:8, :72]


def core_call(*args):
    sd = jax.ShapeDtypeStruct
    V = pltpu.VMEM
    DMA = pltpu.SemaphoreType.DMA
    hbm = [sd((2,) + f, BF) for f in FULL]
    hbm += [sd((2, 2, HW, QW), BF), sd((2, 2, HW, HW), BF), sd((2, 2, HW, D), BF), sd((2, D, 768), BF)]
    hbm += [sd((2, 3, 4 * f[0], f[1]), BF) for f in SLAB]
    hbm += [sd((2, 3) + f, BF) for f in SLAB]
    out = pl.pallas_call(
        core_kernel,
        out_shape=[sd((2, T, D), BF), sd((2, T, D), BF), sd((4, 8, D), F32),
                   sd((4, 32, QW), BF), sd((4, 32, HW), BF), sd((4, 32, D), BF), sd((2, 96, 768), BF)] + hbm,
        in_specs=[VM] * 2 + [pl.BlockSpec(memory_space=pltpu.SMEM)] * 2 + [VM] * 14,
        out_specs=[VM] * 7 + [ANY] * 16,
        scratch_shapes=[
            V((D, QW), BF), V((HW, D), BF), V((D, D), BF), V((D, D), BF),
            V((D, QW), BF), V((HW, D), BF), V((D, D), BF), V((D, D), BF),
            V((2, TG, D), BF), V((2, TG, D), BF), V((TG, D), BF), V((TG, D), BF),
            V((2, TG, QW), BF), V((2, 3, TG, TG), F32), V((2, TG, HW), BF),
            V((2, TG, D), F32), V((2, TG, D), BF),
            V((2, T, D), F32), V((2, T, D), F32), V((2, T, 128), F32), V((2, T, 128), F32),
            V((TG, D), F32), V((3, T, D), BF), V((2, 3, T, D), BF),
            V((TG, D), BF), V((TG, QW), BF), V((TG, HW), BF), V((TG, TG), F32), V((4, 8, 128), F32),
            V((T, D), F32), V((2, T, D), BF),
            V((4, 32, QW), BF), V((4, 32, HW), BF), V((4, 32, D), BF),
            V((2, 2, 32, QW), BF), V((2, 2, 32, HW), BF), V((2, 2, 32, D), BF), V((2, 96, 768), BF),
            V((2, 48, QW), BF), V((2, 48, HW), BF), V((2, 48, D), BF),
            V((2, 96, 768), BF),
            V((768, D), BF), V((576, D), BF), V((2, 64, 8, 128), F32), V((2, 8, D), F32), V((5, 8, D), F32), V((3, 3, 8, D), F32),
            DMA((16, 2)), DMA((16, 4)), DMA((4,)), DMA((4,)), DMA((4,)), DMA((3,)), DMA((3,)),
            DMA((3, 4)), DMA((2,)), DMA((3, 2, 2)), DMA((2,)), DMA((4, 3)), DMA((4, 3)),
            DMA((2, 4)), DMA((2, 4)), DMA((2, 4)), DMA((2, 2, 4)), DMA((2, 4)), DMA((2, 4)), DMA((2, 4)),
            DMA((2, 4)), DMA((2, 4)), DMA((2, 4)), DMA((2, 4)), DMA((2, 4)), DMA((2, 4)), DMA((8,)),
            DMA((2, 4, 2)), DMA((4, 4)), DMA((4, 3)), DMA((4, 3)), DMA((6,)), DMA((6,)), pltpu.SemaphoreType.REGULAR, DMA((2, 4)), DMA((2, 4)), DMA((4,)),
        ],
        compiler_params=pltpu.CompilerParams(collective_id=1, has_side_effects=True,
                                             vmem_limit_bytes=64 * 2**20 - 2**16),
    )(*args)
    return out[:7]


def finish_call(*args):
    def sd(*shape):
        return jax.ShapeDtypeStruct(shape, F32)
    rows = jax.ShapeDtypeStruct((1, 2, 1, T, D), BF)
    row = sd(1, 24)
    return pl.pallas_call(
        finish_kernel,
        out_shape=[rows, rows, row, row, sd(1, 24, 3 * D), sd(1, 72), sd(1, 24, D), row, row, row,
                   sd(1, 24, 4 * D), sd(1, 96), sd(1, 96, D), row],
        in_specs=[VM] * 7,
        out_specs=[VM] * 14,
        compiler_params=pltpu.CompilerParams(vmem_limit_bytes=64 * 2**20 - 2**16),
    )(*args)


def rotary():
    half = 64
    rates = (np.float32(10000.0) ** (-np.arange(half, dtype=np.float32) / np.float32(half))).astype(np.float32)
    ang = np.arange(T, dtype=np.float32)[:, None] * rates[None, :]
    cos, sin = np.cos(ang), np.sin(ang)
    cos2 = np.concatenate([cos, cos], axis=1)
    sin2 = np.concatenate([-sin, sin], axis=1)
    return np.tile(cos2, (4, 1)).astype(np.float32), np.tile(sin2, (4, 1)).astype(np.float32)


def per_device(window_input, cotangent, lengths, widths, gain_first, shift_first, project_weight, project_bias,
               output_weight, output_bias, gain_second, shift_second, expand_weight, expand_bias,
               shrink_weight, shrink_bias):
    cos2, sin2 = rotary()
    parts = core_call(
        window_input[:, 0], cotangent[:, 0], lengths, widths, gain_first, shift_first, output_bias, gain_second,
        shift_second, shrink_bias, expand_bias, project_bias, jnp.asarray(cos2), jnp.asarray(sin2),
        project_weight, output_weight, expand_weight, shrink_weight)
    return tuple(finish_call(*parts))


def solution(mesh):
    row = P("section", "dp")
    mat = P("section", "dp", None)
    params = (row, row, mat, row, mat, row, row, row, mat, row, mat, row)
    seq = P(None, "dp", None, None)
    out = P("section", None, "dp", None, None)
    return jax.shard_map(
        per_device, mesh=mesh,
        in_specs=(seq, seq, P(None, "dp"), P()) + params,
        out_specs=(out, out) + params,
        check_vma=False,
    )
```

time: 358 us -> 273 us (0.76)
  Pallas kernels: 331 us -> 270 us
  local copies, waits for them, and re-layouts: 17.4 us -> 1.3 us
  other arithmetic: 4.35 us -> 0 us
    pallas_call x1, Pallas kernels: 331 us -> 267 us  [core_call(): pl.pallas_call(core_kernel, out_shape=[sd((2, T, D), BF), sd((2, T, D), B...]
    reshape x10 -> x0, local copies, waits for them, and re-layouts: 5.55 us -> none  [the longest x2 1.74 us: per_device(): d_sw = fs.astype(F32).transpose(1, 0, 2).reshape(1, 96, D)]
    pad x8 -> x0, local copies, waits for them, and re-layouts: 5.29 us -> none  [per_device(): jnp.pad(v, ((0, 0), (0, 128 - v.shape[1])))]
where the time goes in v2:
time: 273 us; the launch traced here: 272 us
  Pallas kernels  270 us (99%)
    pallas_call x1, Pallas kernels, core_call(): pl.pallas_call(core_kernel, out_shape=[sd((2, T, D), BF), sd((2, T, D), B...  267 us

profile of v2, /device:TPU:32, one launch (start us, length us, event | category | flops | bytes accessed | tf_op | source)
XLA Modules:
  0.0 271.7 jit_solution(1023322070307925097)
XLA Ops:
  0.6 1.3 copy.32.len_ref
  1.9 266.6 %shard_map.281 = (bf16[2,64,1536]{2,1,0:T(8,128)(2,1)}, bf16[2,64,1536]{2,1,0:T(8,128)(2,1)}, f32[4,8,1536]{2,1,0:T(8,128)}, bf16[4,32,1152]{2,1,0:T(8,128)(2,1)...) custom-call(bf16[2,64,1536]{2,1,0:T(8,128)(2,1)} %bitcast.2, ...), custom_call_target="tpu_custom_call" | custom-call | tf_op jit(solution)/shard_map/pallas_call | solution.py:1033
  268.6 3.1 %shard_map.282 = (bf16[1,2,1,64,1536]{4,3,2,1,0:T(8,128)(2,1)}, bf16[1,2,1,64,1536]{4,3,2,1,0:T(8,128)(2,1)}, f32[1,24]{1,0:T(1,128)}, f32[1,24]{1,0:T(1,128)}, ...) custom-call(bf16[2,64,1536]{2,1,0:T(8,128)(2,1)} %get-tuple-element., ...), custom_call_target="tpu_custom_call" | custom-call | tf_op jit(solution)/shard_map/pallas_call | solution.py:1071

commit v3 on v2

--- a/solution.py
+++ b/solution.py
@@ -21,6 +21,7 @@
 SCALE = 128 ** -0.5
 GC = (2 / np.pi) ** 0.5
 PR, OU, EX, SH = range(4)
+PARTS = (4, 5, 6)
 FULL = ((D, QW), (HW, D), (D, D), (D, D))
 SLAB = ((48, QW), (48, HW), (48, D), (96, 768))
 
@@ -104,19 +105,25 @@
     def ypeer(d):
         return dev(s, (y + d) % 4, x, z)
 
-    a_me = jnp.where(first, x, z)
-    b_me = jnp.where(first, z, x)
-
-    def grid(a, b):
-        return jnp.where(first, a, b), jnp.where(first, b, a)
-
-    def apeer(d):
-        cx, cz = grid((a_me + d) % 4, b_me)
-        return dev(s, y, cx, cz)
-
-    def bpeer(d):
-        cx, cz = grid(a_me, (b_me + d) % 4)
-        return dev(s, y, cx, cz)
+    class Axes:
+        def __init__(self, straight):
+            self.straight = straight
+            self.a, self.b = self.grid(x, z)
+
+        def grid(self, a, b):
+            return jnp.where(self.straight, a, b), jnp.where(self.straight, b, a)
+
+        def apeer(self, d):
+            cx, cz = self.grid((self.a + d) % 4, self.b)
+            return dev(s, y, cx, cz)
+
+        def bpeer(self, d):
+            cx, cz = self.grid(self.a, (self.b + d) % 4)
+            return dev(s, y, cx, cz)
+
+    crossed, same = Axes(first), Axes(False)
+    gather_axes = (crossed, same, crossed, crossed, crossed, crossed, crossed)
+    sum_axes = (crossed, crossed, crossed, crossed)
 
     sib = dev(1 - s, y, x, z)
     own = at(t * T, T, T)
@@ -154,32 +161,31 @@
     r2 = (r2p, r2o, r2e, r2s)
 
     def slab_at(k, j, cx, cz):
-        if k in (PR, EX):
-            return at(48 * (8 * (2 * (cz % 2) + j) + 2 * cx + cz // 2), 48, 48), slice(None)
+        if k not in (OU, SH):
+            half = 1 - cz % 2 if k == EX else cz % 2
+            return at(48 * (8 * (2 * half + j) + 2 * cx + cz // 2), 48, 48), slice(None)
         if k == OU:
             return at(48 * (2 * cx + cz // 2), 48, 48), at(HW * (2 * (cz % 2) + j), HW, HW)
         return at(96 * (4 * cx + cz), 96, 96), at(768 * j, 768, 768)
 
-    def slab_of(ref, k, a, b):
-        cx, cz = grid(a, b)
+    def slab_of(ref, k, axes, a, b):
+        cx, cz = axes.grid(a, b)
         return ref.at[slab_at(k, s, cx, cz)]
 
     def parts_of(ref, k, j):
-        if k in (PR, EX):
+        if k not in (OU, SH):
             return [ref.at[at(HW * (2 * p + j), HW, HW)] for p in (0, 1)]
         if k == OU:
             return [ref.at[:, at(HW * (2 * p + j), HW, HW)] for p in (0, 1)]
         return [ref.at[:, at(768 * j, 768, 768)]]
 
     def bulk(ref, k, slabs):
-        if k in (PR, EX):
-            return ref.at[pl.ds(0, 48 * slabs)]
         if k == OU:
             return ref.at[pl.ds(0, 12 * slabs)] if slabs > 3 else ref.at[pl.ds(0, 144), pl.ds(0, HW)]
         return ref.at[pl.ds(0, 48 * slabs)]
 
-    def piece_target(yt):
-        return dev(y % 2, yt, x, 2 * zh + y // 2), (yt == y) & (s == y % 2) & (zp == y // 2)
+    def piece_target(yt, half):
+        return dev(y % 2, yt, x, 2 * zh + half), (yt == y) & (s == y % 2) & (zp == half)
 
     def out_target(q):
         return dev(q % 2, y, x, 2 * zh + q // 2), (zp == q // 2) & (s == q % 2)
@@ -201,13 +207,13 @@
     def shard_moves():
         out = []
         for yt in range(4):
-            who, me = piece_target(yt)
+            who, me = piece_target(yt, y // 2)
             out.append((sp.at[yt], cp.at[s, zp], z_s.at[0, yt], z_r.at[0, s, zp], who, me))
         for q in range(4):
             who, me = out_target(q)
             out.append((so.at[q], co.at[s, zp], z_s.at[1, q], z_r.at[1, s, zp], who, me))
         for yt in range(4):
-            who, me = piece_target(yt)
+            who, me = piece_target(yt, 1 - y // 2)
             out.append((se.at[yt], ce.at[s, zp], z_s.at[2, yt], z_r.at[2, s, zp], who, me))
         for j in range(2):
             out.append((sw.at[0, :, pl.ds(768 * j, 768)], cs.at[s], zo_s.at[j], zs_r.at[s],
@@ -223,19 +229,20 @@
         for yt in range(4):
             se[yt] = to32(ew[0, :, D * yt:D * (yt + 1)])
 
-    allp[s, pl.ds(chip, 1)] = jnp.zeros((1, 8, 128), F32)
+    spot = (chip % 16) * 4 + y
+    allp[s, pl.ds(spot, 1)] = jnp.zeros((1, 8, 128), F32)
     for r, v in enumerate((v0, v1, v2, v3, v4, v5, v6, v7)):
-        allp[s, pl.ds(chip, 1), r:r + 1, 0:v.shape[1]] = v[...].astype(F32)[None]
+        allp[s, pl.ds(spot, 1), r:r + 1, 0:v.shape[1]] = v[...].astype(F32)[None]
 
     def pack_copies(stage):
         out = []
         for d in (1, 2, 3):
             if stage == 0:
-                blk, who = allp.at[s, pl.ds(chip, 1)], dev(s, y, x, (z + d) % 4)
+                blk, who = allp.at[s, pl.ds(spot, 1)], ypeer(d)
             elif stage == 1:
-                blk, who = allp.at[s, at(chip - z, 4, 4)], dev(s, y, (x + d) % 4, z)
+                blk, who = allp.at[s, at(spot - y, 4, 4)], dev(s, y, x, (z + d) % 4)
             else:
-                blk, who = allp.at[s, at(16 * y, 16, 16)], ypeer(d)
+                blk, who = allp.at[s, at(16 * x, 16, 16)], dev(s, y, (x + d) % 4, z)
             out.append(remote(blk, blk, p_s.at[stage, d - 1], p_r.at[stage, d - 1], who))
         return out
 
@@ -249,7 +256,7 @@
         for c in pack_copies(stage):
             c.wait()
 
-    length = len_ref[s, 0].astype(F32)
+    length = len_ref[s].astype(F32)
     width = wid_ref[s]
     lens[pl.ds(t, 1)] = jnp.full((1, 8, 128), length, F32)
     lcs = [remote(lens.at[pl.ds(t, 1)], lens.at[pl.ds(t, 1)], l_s.at[d - 1], l_r.at[d - 1], ypeer(d)) for d in (1, 2, 3)]
@@ -258,15 +265,22 @@
     bld = (bp, bo, be, cs)
 
     def home(l, k):
+        if k in PARTS:
+            return w_v[PR].at[:, pl.ds(HW * (k - 4), HW)]
         return w_hbm[k].at[1] if l else w_v[k]
 
+    def slab_in(l, k):
+        return bld[PR].at[l, :, pl.ds(HW * (k - 4), HW)] if k in PARTS else bld[k].at[l]
+
     def a_copies(l, k):
-        src = bld[k].at[l]
-        return [remote(src, slab_of(home(l, k), k, a_me, b_me), a_s.at[l, k], a_r.at[l, k], apeer(d))
+        src = slab_in(l, k)
+        ax = gather_axes[k]
+        return [remote(src, slab_of(home(l, k), k, ax, ax.a, ax.b), a_s.at[l, k], a_r.at[l, k], ax.apeer(d))
                 for d in (1, 2, 3)]
 
     def own_copy(l, k):
-        return pltpu.make_async_copy(bld[k].at[l], slab_of(home(l, k), k, a_me, b_me), o_sem.at[l, k])
+        ax = gather_axes[k]
+        return pltpu.make_async_copy(slab_in(l, k), slab_of(home(l, k), k, ax, ax.a, ax.b), o_sem.at[l, k])
 
     @named("gather a")
     def gather_a(l, k):
@@ -278,28 +292,28 @@
                 wait_for(got[k].at[l, p], z_r.at[zk, l, p])
             halves = [got[k][l, p].astype(F32)[:24] for p in (0, 1)]
             bld[k][l] = jnp.concatenate(halves, axis=0).astype(BF)
-        for c in a_copies(l, k):
-            c.start()
-        own_copy(l, k).start()
+        for item in PARTS if (l, k) == (0, PR) else (k,):
+            go(a_copies(l, item))
+            own_copy(l, item).start()
 
     @named("gather b")
     def gather_b(l, k):
-        w = home(l, k)
+        w, ax = home(l, k), gather_axes[k]
         wait_for(bulk(w, k, 3), a_r.at[l, k])
         own_copy(l, k).wait()
         for a in range(4):
-            src = slab_of(w, k, a, b_me)
+            src = slab_of(w, k, ax, a, ax.b)
             for side, d in ((0, 1), (1, 3)):
-                remote(src, src, b_s.at[l, k], b_r.at[side, l, k], bpeer(d)).start()
+                remote(src, src, b_s.at[l, k], b_r.at[side, l, k], ax.bpeer(d)).start()
 
     @named("gather f")
     def gather_f(l, k):
-        w = home(l, k)
+        w, ax = home(l, k), gather_axes[k]
         for side, d in ((0, 1), (1, 3)):
             wait_for(bulk(w, k, 4), b_r.at[side, l, k])
             for a in (2 * side, 2 * side + 1):
-                src = slab_of(w, k, a, (b_me + 4 - d) % 4)
-                remote(src, src, b_s.at[l, k], f2_r.at[l, k], bpeer(d)).start()
+                src = slab_of(w, k, ax, a, (ax.b + 4 - d) % 4)
+                remote(src, src, b_s.at[l, k], f2_r.at[l, k], ax.bpeer(d)).start()
 
     @named("gather c")
     def gather_c(l, k):
@@ -311,22 +325,25 @@
     @named("gather d")
     def gather_d(l, k):
         wait_for(bulk(home(l, k), k, 16), c_r.at[l, k])
-        if l == 0:
-            save(k).start()
+        if l == 0 and k not in (4, 5):
+            save(PR if k == 6 else k).start()
 
     def save(k):
         return pltpu.make_async_copy(w_v[k], w_hbm[k].at[0], v_sem.at[k])
 
     @named("gather drain")
     def gather_drain(l, k):
-        w = home(l, k)
-        wait_for(bulk(w, k, 3), a_s.at[l, k])
-        wait_for(bulk(w, k, 12), b_s.at[l, k])
-        wait_for(bulk(w, k, 16), c_s.at[l, k])
+        for item in PARTS if (l, k) == (0, PR) else (k,):
+            w = home(l, item)
+            wait_for(bulk(w, item, 3), a_s.at[l, item])
+            wait_for(bulk(w, item, 12), b_s.at[l, item])
+            wait_for(bulk(w, item, 16), c_s.at[l, item])
 
     def gbuf(l, k):
         if l == 0 and k == PR:
             return us_.at[:, pl.ds(0, QW)]
+        if l == 0 and k == SH:
+            return ue
         return g_v[k] if l else w_v[k]
 
     @named("sum0 go")
@@ -354,7 +371,7 @@
 
     @named("sum0")
     def sum0_fin(l, k):
-        g = gbuf(l, k)
+        g, ax = gbuf(l, k), sum_axes[k]
         cps = sum0_copies(l, k)
         for p in (0, 1):
             cps[p].wait()
@@ -373,11 +390,12 @@
             tiles(8 if k == SH else 4, add)
         for a in (0, 2, 1, 3):
             far = 1 if a < 2 else 3
-            remote(slab_of(g, k, a, (b_me + 2) % 4), r1_slab(l, k, 0, a), q1_s.at[l, k], qf_r.at[l, k], bpeer(far)).start()
+            remote(slab_of(g, k, ax, a, (ax.b + 2) % 4), r1_slab(l, k, 0, a), q1_s.at[l, k], qf_r.at[l, k],
+                   ax.bpeer(far)).start()
         for a in (0, 2, 1, 3):
             near = 3 if a < 2 else 1
-            remote(slab_of(g, k, a, (b_me + near) % 4), r1_slab(l, k, near, a), q1_s.at[l, k], q1_r.at[l, k],
-                   bpeer(near)).start()
+            remote(slab_of(g, k, ax, a, (ax.b + near) % 4), r1_slab(l, k, near, a), q1_s.at[l, k], q1_r.at[l, k],
+                   ax.bpeer(near)).start()
 
     def r1_slab(l, k, d, a):
         rows = SLAB[k][0]
@@ -395,37 +413,57 @@
             return tmp1[at(rows * a, rows, rows), cols * side:cols * (side + 1)].astype(F32)
         return tmp1[at(4 * rows * side + rows * a, rows, rows), 0:cols].astype(F32)
 
+    def mid_copies(l, k):
+        rows, cols = SLAB[k]
+        if k != SH:
+            return [pltpu.make_async_copy(r1[k].at[l, 0], tmp1.at[pl.ds(384, 192), pl.ds(0, cols)], t_sem.at[2])]
+        return [pltpu.make_async_copy(r1[k].at[l, 0, pl.ds(192 * i, 192)], tmp1.at[pl.ds(384, 192), pl.ds(768 * i, 768)],
+                                      t_sem.at[(2, 8)[i]]) for i in (0, 1)]
+
+    def mid_slab(k, a):
+        rows, cols = SLAB[k]
+        if k != SH:
+            return tmp1[384 + 48 * a:432 + 48 * a, 0:cols].astype(F32)
+        return tmp1[384 + 96 * (a % 2):480 + 96 * (a % 2), 768 * (a // 2):768 * (a // 2) + 768].astype(F32)
+
+    @named("sum1 pass load")
+    def mid_load(l, k):
+        wait_for(r1[k].at[l, 0], qf_r.at[l, k])
+        go(mid_copies(l, k))
+
     @named("sum1 pass on")
-    def sum1_mid(l, k):
-        g = gbuf(l, k)
-        wait_for(r1[k].at[l, 0], qf_r.at[l, k])
-        c = pltpu.make_async_copy(r1[k].at[l, 0], tmp_set(k, 0), t_sem.at[2])
-        c.start()
-        c.wait()
+    def mid_fin(l, k):
+        g, ax = gbuf(l, k), sum_axes[k]
+        end(mid_copies(l, k))
         for a in range(4):
             d = 1 if a < 2 else 3
-            cx, cz = grid(a, (b_me + d) % 4)
+            cx, cz = ax.grid(a, (ax.b + d) % 4)
             where = slab_at(k, s, cx, cz)
-            g[where] = (g[where].astype(F32) + tmp_slab(k, 0, a)).astype(BF)
-            remote(g.at[where], r1_slab(l, k, d, a), q1_s.at[l, k], q1_r.at[l, k], bpeer(d)).start()
+            g[where] = (g[where].astype(F32) + mid_slab(k, a)).astype(BF)
+            remote(g.at[where], r1_slab(l, k, d, a), q1_s.at[l, k], q1_r.at[l, k], ax.bpeer(d)).start()
+
+    def last_copies(l, k):
+        return [pltpu.make_async_copy(r1[k].at[l, 1 + i], tmp_set(k, i), t_sem.at[3 + i]) for i in (0, 1)]
+
+    @named("sum1 load")
+    def last_load(l, k):
+        wait_for(r1[k].at[l, pl.ds(1, 2)], q1_r.at[l, k])
+        go(last_copies(l, k))
 
     @named("sum1")
-    def sum1_end(l, k):
-        g = gbuf(l, k)
-        wait_for(r1[k].at[l, pl.ds(1, 2)], q1_r.at[l, k])
-        cps = [pltpu.make_async_copy(r1[k].at[l, 1 + i], tmp_set(k, i), t_sem.at[3 + i]) for i in (0, 1)]
-        go(cps)
-        end(cps)
+    def last_fin(l, k):
+        g, ax = gbuf(l, k), sum_axes[k]
+        end(last_copies(l, k))
         for da in (2, 1, 3, 0):
-            a = (a_me + da) % 4
-            cx, cz = grid(a, b_me)
+            a = (ax.a + da) % 4
+            cx, cz = ax.grid(a, ax.b)
             where = slab_at(k, s, cx, cz)
             total = g[where].astype(F32) + tmp_slab(k, 0, a) + tmp_slab(k, 1, a)
             if da == 0:
                 bld[k][l] = total.astype(BF)
             else:
                 g[where] = total.astype(BF)
-                remote(g.at[where], r2[k].at[l, da - 1], q2_s.at[l, k], q2_r.at[l, k], apeer(da)).start()
+                remote(g.at[where], r2[k].at[l, da - 1], q2_s.at[l, k], q2_r.at[l, k], ax.apeer(da)).start()
 
     fsend = (sp, so, se, fss)
     frecv = (fp, fo, fe, fs)
@@ -440,7 +478,7 @@
                 q = 2 * zp + s
                 who, me, slot = dev(l, y, x, 2 * zh + p), (s == l) & (zp == p), q
             else:
-                yo = 2 * zp + s
+                yo = 2 * (zp if k == PR else 1 - zp) + s
                 who, me, slot = dev(l, yo, x, 2 * zh + p), (s == l) & (yo == y) & (zp == p), y
             out.append((fsend[k].at[2 * l + p], frecv[k].at[slot], f_s.at[l, k, p], f_r.at[k, slot], who, me))
         return out
@@ -487,9 +525,9 @@
             return out
         for d in (1, 2, 3):
             if stage == 1:
-                who = apeer(d)
+                who = crossed.apeer(d)
             elif stage == 2:
-                who = bpeer(d)
+                who = crossed.bpeer(d)
             else:
                 out.append(remote(sm_out.at[t], sm_out.at[t], e_s.at[3, d - 1], e_r.at[3, d - 1], ypeer(d)))
                 continue
@@ -618,6 +656,8 @@
             wcopy(PR, 1).wait()
         with jax.named_scope("queries keys values"):
             for part in range(3):
+                if l == 0:
+                    gather_d(0, PARTS[part])
                 joined = nn(normed[l], vp[:, part * HW:(part + 1) * HW]) + small[l, 7:8, part * HW:(part + 1) * HW]
                 for h in range(3):
                     v = joined[:, h * 128:(h + 1) * 128]
@@ -718,6 +758,8 @@
             gbuf(l, EX)[c, :] = tn(ns[l, :, c], dup[...]).astype(BF)
 
         if l == 0:
+            tiles(6, gs_tile)
+            sum0_go(0, SH)
             wcopy(SH, 0).wait()
             tiles(6, dact_tile)
             wcopy(EX, 0).wait()
@@ -734,9 +776,7 @@
         reduce_go(4 + l * 2, "e_tile", lambda c: nt(dup[...], ve[c, :]))
         if l == 1:
             wcopy(EX, 0).start()
-        else:
-            tiles(6, gs_tile)
-            sum0_go(0, SH)
+        hook("partial")
         tiles(6, ge_tile)
         sum0_go(l, EX)
         hook("upper")
@@ -781,11 +821,14 @@
         if l == 0:
             wcopy(PR, 0).wait()
 
+        hook("scores")
+
         def gp_tile(i):
             c = span(i, 256)
             gbuf(l, PR)[c, :] = tn(normed[l, :, c], dj[...]).astype(BF)
         tiles(6, gp_tile)
         sum0_go(l, PR)
+        hook("project")
         reduce_go(4 + l * 2 + 1, "d_tile", lambda c: nt(dj[...], vp[c, :]))
         if l == 1:
             wcopy(PR, 0).start()
@@ -806,6 +849,7 @@
 
     hall = dball
     hall[own, :] = win_ref[s]
+    gall[own, :] = (cot_ref[s].astype(F32) * livef).astype(BF)
     h_cps = [remote(hall.at[own], hall.at[own], m_s.at[d - 1], m_r.at[d - 1], ypeer(d)) for d in (1, 2, 3)]
     g_cps = [remote(gall.at[own], gall.at[own], m_s.at[2 + d], m_r.at[2 + d], ypeer(d)) for d in (1, 2, 3)]
     pack_last = remote(allp.at[s], allp.at[s], p_s.at[3, 0], p_r.at[3, 0], sib)
@@ -818,8 +862,10 @@
     def _():
         for m in moves[:4]:
             send_or_keep(*m)
+    gather_a(0, PR)
+    pack_end(0)
+    pack_go(1)
     go(h_cps)
-    gather_a(0, PR)
 
     @pl.when(first)
     def _():
@@ -827,12 +873,20 @@
             send_or_keep(*m)
     for m in moves[12:]:
         send_or_keep(*m)
-    pack_end(0)
-    pack_go(1)
-    gather_b(0, PR)
-    gather_a(0, OU)
+    for k in PARTS:
+        gather_b(0, k)
+
+    @pl.when(first)
+    def _():
+        for m in moves[8:12]:
+            send_or_keep(*m)
     pack_end(1)
     pack_go(2)
+    gather_a(0, OU)
+    for k in PARTS:
+        gather_f(0, k)
+    gather_b(0, OU)
+    go(g_cps)
     end(lcs)
     row = lax.broadcasted_iota(jnp.int32, (TG, TG), 0)
     col = lax.broadcasted_iota(jnp.int32, (TG, TG), 1)
@@ -847,57 +901,33 @@
     xh, rsd = stats(hidden0)
     xh1[0] = xh
     rd1[0] = jnp.broadcast_to(rsd, (T, 128))
-    gall[own, :] = (cot_ref[s].astype(F32) * livef).astype(BF)
-    gather_f(0, PR)
-
-    @pl.when(first)
-    def _():
-        for m in moves[8:12]:
-            send_or_keep(*m)
-    gather_b(0, OU)
     pack_end(2)
     pack_last.start()
-    gather_c(0, PR)
     gather_a(0, EX)
-    gather_a(0, SH)
+    for k in PARTS:
+        gather_c(0, k)
     gather_f(0, OU)
-    go(g_cps)
     end(h_cps)
     pack_last.wait()
 
-    def spread(rows, width, total):
-        n = lax.broadcasted_iota(jnp.int32, (128, total), 1)
+    def spread(l, r, width, total, feature):
+        n = feature(lax.broadcasted_iota(jnp.int32, (128, total), 1))
         i = lax.broadcasted_iota(jnp.int32, (128, total), 0)
         pick = jnp.where(n - (n // width) * width == i, 1.0, 0.0).astype(BF)
-        wide = nn(rows.astype(BF), pick)
-        n = lax.broadcasted_iota(jnp.int32, (64, total), 1)
-        c = lax.broadcasted_iota(jnp.int32, (64, total), 0)
-        return colsum(jnp.where(n // width == c, wide, 0.0))
+        wide = nn(allp[l, :, r, :].astype(BF), pick)
+        n = feature(lax.broadcasted_iota(jnp.int32, (64, total), 1))
+        i = lax.broadcasted_iota(jnp.int32, (64, total), 0)
+        small[l, r:r + 1, 0:total] = colsum(jnp.where(n // width == (i % 4) * 16 + i // 4, wide, 0.0))
 
     @named("spread")
     def unpack(l, wanted):
         for r in wanted:
             if r < 6:
-                small[l, r:r + 1, :] = spread(allp[l, :, r, :], 24, D)
+                spread(l, r, 24, D, lambda n: n)
             elif r == 6:
-                mine = allp[l, at(16 * t, 16, 16), 6, :]
-                n = lax.broadcasted_iota(jnp.int32, (128, D), 1)
-                i = lax.broadcasted_iota(jnp.int32, (128, D), 0)
-                pick = jnp.where(n - (n // 96) * 96 == i, 1.0, 0.0).astype(BF)
-                wide = nn(mine.astype(BF), pick)
-                n = lax.broadcasted_iota(jnp.int32, (16, D), 1)
-                c = lax.broadcasted_iota(jnp.int32, (16, D), 0)
-                small[l, 6:7, :] = colsum(jnp.where(n // 96 == c, wide, 0.0))
+                spread(l, r, 96, D, lambda n: n + D * t)
             else:
-                n = lax.broadcasted_iota(jnp.int32, (128, QW), 1)
-                i = lax.broadcasted_iota(jnp.int32, (128, QW), 0)
-                n = n + (n // HW) * (D - HW) + HW * t
-                pick = jnp.where(n - (n // 72) * 72 == i, 1.0, 0.0).astype(BF)
-                wide = nn(allp[l, :, 7, :].astype(BF), pick)
-                n = lax.broadcasted_iota(jnp.int32, (64, QW), 1)
-                c = lax.broadcasted_iota(jnp.int32, (64, QW), 0)
-                n = n + (n // HW) * (D - HW) + HW * t
-                small[l, 7:8, 0:QW] = colsum(jnp.where(n // 72 == c, wide, 0.0))
+                spread(l, r, 72, QW, lambda n: n + (n // HW) * (D - HW) + HW * t)
 
     unpack(0, (0, 1, 7))
 
@@ -906,9 +936,9 @@
         wide, _ = stats(hall[rows, :].astype(F32))
         normed[0, rows, :] = (wide * small[0, 0:1, :] + small[0, 1:2, :]).astype(BF)
     tiles(4, norm_tile)
+    gather_c(0, OU)
     gather_b(0, EX)
-    gather_c(0, OU)
-    gather_d(0, PR)
+    gather_a(0, SH)
 
     def steps(*todo):
         def run():
@@ -936,18 +966,19 @@
                 send_or_keep(*m)
 
     first_hooks = dict(
-        joined=steps((gb, 0, SH), (gd, 0, OU)),
-        mixed=steps((second_first,), (unpack, 0, (2, 3, 4, 5, 6))),
-        mixed2=steps((gf, 0, EX), (second_shards,), (ga, 1, PR), (ga, 1, OU), (gc, 0, EX)),
-        second=steps((gf, 0, SH)),
-        second2=steps((gb, 1, PR), (ga, 1, EX), (gc, 0, SH), (gd, 0, EX)),
-        upper=steps((gb, 1, OU), (gd, 0, SH)),
-        down=steps((unpack, 1, (0, 1, 2, 3, 4, 5, 6, 7)), (ga, 1, SH)),
-        down2=steps((gf, 1, PR), (gb, 1, EX), (gf, 1, OU), (gc, 1, PR)))
+        joined=steps((gd, 0, OU)),
+        mixed=steps((unpack, 0, (2, 3, 4, 5, 6)), (gf, 0, EX), (gb, 0, SH)),
+        mixed2=steps((second_first,), (gc, 0, EX)),
+        second=steps((unpack, 1, (0, 1, 2, 3, 4, 5, 6, 7)), (ga, 1, PR), (ga, 1, OU)),
+        second2=steps((gf, 0, SH), (second_shards,), (gd, 0, EX)),
+        upper=steps((gb, 1, PR), (gb, 1, OU), (gc, 0, SH), (gd, 0, SH)),
+        down=steps((ga, 1, EX), (ga, 1, SH)),
+        down2=steps((gf, 1, PR), (gf, 1, OU), (gb, 1, EX), (gc, 1, PR)))
     second_hooks = dict(
-        normed2=steps((gb, 1, SH), (gc, 1, OU), (gf, 1, EX), (reload, PR)),
+        normed2=steps((gc, 1, OU), (gb, 1, SH), (gf, 1, EX), (reload, PR)),
         joined=steps((reload, OU)),
-        mixed2=steps((gc, 1, EX), (gf, 1, SH)),
+        mixed=steps((gf, 1, SH)),
+        mixed2=steps((gc, 1, EX)),
         second2=steps((gc, 1, SH), (reload, EX)),
         upper=steps((reload, SH)))
     a1 = forward(0, hidden0, first_hooks)
@@ -958,34 +989,44 @@
     for m in moves:
         sent(*m)
 
-    load, fin, mid, last = sum0_load, sum0_fin, sum1_mid, sum1_end
+    load, fin, ml, mf, ll, lf = sum0_load, sum0_fin, mid_load, mid_fin, last_load, last_fin
+
+    def mid(l, k):
+        mid_load(l, k)
+        mid_fin(l, k)
+
+    def last(l, k):
+        last_load(l, k)
+        last_fin(l, k)
+
     ig2 = backward(1, gall[own, :], dict(
         result2=steps((load, 1, SH), (fin, 1, SH)),
-        upper2=steps((mid, 1, SH), (load, 1, EX), (fin, 1, EX)),
-        middle2=steps((last, 1, SH), (mid, 1, EX)),
+        upper2=steps((ml, 1, SH), (load, 1, EX), (mf, 1, SH), (fin, 1, EX)),
+        middle2=steps((ll, 1, SH), (ml, 1, EX), (mf, 1, EX), (lf, 1, SH)),
         joined=steps((load, 1, PR), (fin, 1, PR)),
-        joined2=steps((load, 1, OU), (last, 1, EX), (fin, 1, OU))))
+        joined2=steps((load, 1, OU), (ll, 1, EX), (fin, 1, OU), (lf, 1, EX))))
     g1 = (ig2.astype(F32) * livef).astype(BF)
     backward(0, g1, dict(
         grad=steps((sum2_end, 1, SH), (sum_drain, 1, SH)),
-        grad2=steps((mid, 1, PR), (mid, 1, OU), (sum2_end, 1, EX)),
-        upper2=steps((load, 0, SH), (last, 1, PR), (fin, 0, SH)),
-        middle=steps((load, 0, EX), (last, 1, OU), (fin, 0, EX)),
-        middle2=steps((mid, 0, SH), (sum2_end, 1, PR)),
-        joined=steps((load, 0, PR), (fin, 0, PR)),
-        joined2=steps((load, 0, OU), (mid, 0, EX), (fin, 0, OU), (last, 0, SH))))
+        grad2=steps((ml, 1, PR), (mf, 1, PR), (mid, 1, OU), (sum_drain, 1, EX)),
+        partial=steps((load, 0, SH), (fin, 0, SH)),
+        upper2=steps((ll, 1, PR), (ml, 0, SH), (lf, 1, PR), (mf, 0, SH)),
+        middle=steps((load, 0, EX), (ll, 1, OU), (fin, 0, EX), (lf, 1, OU)),
+        middle2=steps((sum2_end, 1, EX), (sum2_end, 1, PR)),
+        project=steps((ml, 0, EX), (mf, 0, EX)),
+        joined=steps((load, 0, PR), (ll, 0, SH), (fin, 0, PR), (lf, 0, SH)),
+        joined2=steps((load, 0, OU), (fin, 0, OU), (last, 0, EX))))
     vec_go(0)
+    mid(0, PR)
     vec_end(0)
     vec_go(1)
-    last(0, EX)
-    mid(0, PR)
     mid(0, OU)
-    sum2_end(1, OU)
     sum2_end(0, SH)
+    last(0, PR)
     vec_end(1)
     vec_go(2)
-    last(0, PR)
     last(0, OU)
+    sum2_end(1, OU)
     sum2_end(0, EX)
     vec_end(2)
     vec_go(3)
@@ -996,7 +1037,7 @@
     finish_results()
     for k in range(4):
         for l in (0, 1):
-            if (l, k) != (1, SH):
+            if (l, k) not in ((1, SH), (1, EX)):
                 sum_drain(l, k)
 
 
@@ -1053,9 +1094,9 @@
             V((768, D), BF), V((576, D), BF), V((2, 64, 8, 128), F32), V((2, 8, D), F32), V((5, 8, D), F32), V((3, 3, 8, D), F32),
             DMA((16, 2)), DMA((16, 4)), DMA((4,)), DMA((4,)), DMA((4,)), DMA((3,)), DMA((3,)),
             DMA((3, 4)), DMA((2,)), DMA((3, 2, 2)), DMA((2,)), DMA((4, 3)), DMA((4, 3)),
-            DMA((2, 4)), DMA((2, 4)), DMA((2, 4)), DMA((2, 2, 4)), DMA((2, 4)), DMA((2, 4)), DMA((2, 4)),
-            DMA((2, 4)), DMA((2, 4)), DMA((2, 4)), DMA((2, 4)), DMA((2, 4)), DMA((2, 4)), DMA((8,)),
-            DMA((2, 4, 2)), DMA((4, 4)), DMA((4, 3)), DMA((4, 3)), DMA((6,)), DMA((6,)), pltpu.SemaphoreType.REGULAR, DMA((2, 4)), DMA((2, 4)), DMA((4,)),
+            DMA((2, 7)), DMA((2, 7)), DMA((2, 7)), DMA((2, 2, 7)), DMA((2, 7)), DMA((2, 7)), DMA((2, 7)),
+            DMA((2, 4)), DMA((2, 4)), DMA((2, 4)), DMA((2, 4)), DMA((2, 4)), DMA((2, 4)), DMA((9,)),
+            DMA((2, 4, 2)), DMA((4, 4)), DMA((4, 3)), DMA((4, 3)), DMA((6,)), DMA((6,)), pltpu.SemaphoreType.REGULAR, DMA((2, 7)), DMA((2, 4)), DMA((4,)),
         ],
         compiler_params=pltpu.CompilerParams(collective_id=1, has_side_effects=True,
                                              vmem_limit_bytes=64 * 2**20 - 2**16),
@@ -1093,7 +1134,7 @@
                shrink_weight, shrink_bias):
     cos2, sin2 = rotary()
     parts = core_call(
-        window_input[:, 0], cotangent[:, 0], lengths, widths, gain_first, shift_first, output_bias, gain_second,
+        window_input[:, 0], cotangent[:, 0], lengths.reshape(2), widths, gain_first, shift_first, output_bias, gain_second,
         shift_second, shrink_bias, expand_bias, project_bias, jnp.asarray(cos2), jnp.asarray(sin2),
         project_weight, output_weight, expand_weight, shrink_weight)
     return tuple(finish_call(*parts))

time: 273 us -> 264 us (0.967)
  Pallas kernels: 270 us -> 262 us
    pallas_call x1, Pallas kernels: 267 us -> 259 us  [core_call(): pl.pallas_call(core_kernel, out_shape=[sd((2, T, D), BF), sd((2, T, D), B...]
where the time goes in v3:
time: 264 us; the launch traced here: 263 us
  Pallas kernels  262 us (99%)
    pallas_call x1, Pallas kernels, core_call(): pl.pallas_call(core_kernel, out_shape=[sd((2, T, D), BF), sd((2, T, D), B...  259 us

profile of v3, /device:TPU:32, one launch (start us, length us, event | category | flops | bytes accessed | tf_op | source)
XLA Modules:
  0.0 262.8 jit_solution(17138043704590902398)
XLA Ops:
  0.7 259.0 %shard_map.281 = (bf16[2,64,1536]{2,1,0:T(8,128)(2,1)}, bf16[2,64,1536]{2,1,0:T(8,128)(2,1)}, f32[4,8,1536]{2,1,0:T(8,128)}, bf16[4,32,1152]{2,1,0:T(8,128)(2,1)...) custom-call(bf16[2,64,1536]{2,1,0:T(8,128)(2,1)} %bitcast.3, ...), custom_call_target="tpu_custom_call" | custom-call | tf_op jit(solution)/shard_map/pallas_call | solution.py:1074
  259.7 3.1 %shard_map.282 = (bf16[1,2,1,64,1536]{4,3,2,1,0:T(8,128)(2,1)}, bf16[1,2,1,64,1536]{4,3,2,1,0:T(8,128)(2,1)}, f32[1,24]{1,0:T(1,128)}, f32[1,24]{1,0:T(1,128)}, ...) custom-call(bf16[2,64,1536]{2,1,0:T(8,128)(2,1)} %get-tuple-element., ...), custom_call_target="tpu_custom_call" | custom-call | tf_op jit(solution)/shard_map/pallas_call | solution.py:1112

commit v4 on v3

--- a/solution.py
+++ b/solution.py
@@ -676,6 +676,7 @@
                 p = ex * (1.0 / jnp.sum(ex, axis=-1, keepdims=True))
                 probs[l, h] = p
                 mixed[l, :, h * 128:(h + 1) * 128] = nn(p.astype(BF), v).astype(BF)
+        hook("attended")
         if l:
             wcopy(OU, 1).wait()
         reduce_go(l * 2, "out_tile", lambda c: nn(mixed[l], vo[:, c]))
@@ -886,6 +887,11 @@
     for k in PARTS:
         gather_f(0, k)
     gather_b(0, OU)
+
+    @pl.when(jnp.logical_not(first))
+    def _():
+        for m in moves[:8]:
+            send_or_keep(*m)
     go(g_cps)
     end(lcs)
     row = lax.broadcasted_iota(jnp.int32, (TG, TG), 0)
@@ -936,9 +942,7 @@
         wide, _ = stats(hall[rows, :].astype(F32))
         normed[0, rows, :] = (wide * small[0, 0:1, :] + small[0, 1:2, :]).astype(BF)
     tiles(4, norm_tile)
-    gather_c(0, OU)
     gather_b(0, EX)
-    gather_a(0, SH)
 
     def steps(*todo):
         def run():
@@ -959,26 +963,21 @@
         wcopy(k, 1).start()
 
     ga, gb, gf, gc, gd = gather_a, gather_b, gather_f, gather_c, gather_d
-    def second_first():
-        @pl.when(jnp.logical_not(first))
-        def _():
-            for m in moves[:8]:
-                send_or_keep(*m)
-
     first_hooks = dict(
-        joined=steps((gd, 0, OU)),
+        joined=steps((gc, 0, OU), (ga, 0, SH)),
+        attended=steps((gd, 0, OU)),
         mixed=steps((unpack, 0, (2, 3, 4, 5, 6)), (gf, 0, EX), (gb, 0, SH)),
-        mixed2=steps((second_first,), (gc, 0, EX)),
-        second=steps((unpack, 1, (0, 1, 2, 3, 4, 5, 6, 7)), (ga, 1, PR), (ga, 1, OU)),
-        second2=steps((gf, 0, SH), (second_shards,), (gd, 0, EX)),
-        upper=steps((gb, 1, PR), (gb, 1, OU), (gc, 0, SH), (gd, 0, SH)),
-        down=steps((ga, 1, EX), (ga, 1, SH)),
-        down2=steps((gf, 1, PR), (gf, 1, OU), (gb, 1, EX), (gc, 1, PR)))
+        mixed2=steps((ga, 1, PR), (ga, 1, OU), (gc, 0, EX)),
+        second=steps((unpack, 1, (0, 1, 2, 3, 4, 5, 6, 7))),
+        second2=steps((gf, 0, SH), (gb, 1, PR), (gb, 1, OU), (gd, 0, EX)),
+        upper=steps((gc, 0, SH), (second_shards,), (gd, 0, SH)),
+        down=steps((gf, 1, PR), (gf, 1, OU), (ga, 1, SH)),
+        down2=steps((ga, 1, EX), (gc, 1, PR)))
     second_hooks = dict(
-        normed2=steps((gc, 1, OU), (gb, 1, SH), (gf, 1, EX), (reload, PR)),
+        normed2=steps((gc, 1, OU), (gb, 1, EX), (gb, 1, SH), (reload, PR)),
         joined=steps((reload, OU)),
-        mixed=steps((gf, 1, SH)),
-        mixed2=steps((gc, 1, EX)),
+        mixed=steps((gf, 1, EX)),
+        mixed2=steps((gf, 1, SH), (gc, 1, EX)),
         second2=steps((gc, 1, SH), (reload, EX)),
         upper=steps((reload, SH)))
     a1 = forward(0, hidden0, first_hooks)

time: 264 us -> 263 us (level)
  no operation moved by 1% of the time
where the time goes in v4:
time: 263 us; the launch traced here: 261 us
  Pallas kernels  261 us (99%)
    pallas_call x1, Pallas kernels, core_call(): pl.pallas_call(core_kernel, out_shape=[sd((2, T, D), BF), sd((2, T, D), B...  258 us

profile of v4, /device:TPU:32, one launch (start us, length us, event | category | flops | bytes accessed | tf_op | source)
XLA Modules:
  0.0 261.4 jit_solution(9871557589946965580)
XLA Ops:
  0.7 257.7 %shard_map.281 = (bf16[2,64,1536]{2,1,0:T(8,128)(2,1)}, bf16[2,64,1536]{2,1,0:T(8,128)(2,1)}, f32[4,8,1536]{2,1,0:T(8,128)}, bf16[4,32,1152]{2,1,0:T(8,128)(2,1)...) custom-call(bf16[2,64,1536]{2,1,0:T(8,128)(2,1)} %bitcast.3, ...), custom_call_target="tpu_custom_call" | custom-call | tf_op jit(solution)/shard_map/pallas_call | solution.py:1073
  258.3 3.1 %shard_map.282 = (bf16[1,2,1,64,1536]{4,3,2,1,0:T(8,128)(2,1)}, bf16[1,2,1,64,1536]{4,3,2,1,0:T(8,128)(2,1)}, f32[1,24]{1,0:T(1,128)}, f32[1,24]{1,0:T(1,128)}, ...) custom-call(bf16[2,64,1536]{2,1,0:T(8,128)(2,1)} %get-tuple-element., ...), custom_call_target="tpu_custom_call" | custom-call | tf_op jit(solution)/shard_map/pallas_call | solution.py:1111

commit v5 on v4

--- a/solution.py
+++ b/solution.py
@@ -977,8 +977,9 @@
         normed2=steps((gc, 1, OU), (gb, 1, EX), (gb, 1, SH), (reload, PR)),
         joined=steps((reload, OU)),
         mixed=steps((gf, 1, EX)),
-        mixed2=steps((gf, 1, SH), (gc, 1, EX)),
-        second2=steps((gc, 1, SH), (reload, EX)),
+        mixed2=steps((gc, 1, EX)),
+        second=steps((gf, 1, SH)),
+        second2=steps((reload, EX), (gc, 1, SH)),
         upper=steps((reload, SH)))
     a1 = forward(0, hidden0, first_hooks)
     forward(1, a1.astype(F32), second_hooks)

time: 263 us -> 263 us (level)
  no operation moved by 1% of the time
where the time goes in v5:
time: 263 us; the launch traced here: 261 us
  Pallas kernels  261 us (99%)
    pallas_call x1, Pallas kernels, core_call(): pl.pallas_call(core_kernel, out_shape=[sd((2, T, D), BF), sd((2, T, D), B...  257 us

profile of v5, /device:TPU:32, one launch (start us, length us, event | category | flops | bytes accessed | tf_op | source)
XLA Modules:
  0.0 261.2 jit_solution(46295171295520593)
XLA Ops:
  0.7 257.4 %shard_map.281 = (bf16[2,64,1536]{2,1,0:T(8,128)(2,1)}, bf16[2,64,1536]{2,1,0:T(8,128)(2,1)}, f32[4,8,1536]{2,1,0:T(8,128)}, bf16[4,32,1152]{2,1,0:T(8,128)(2,1)...) custom-call(bf16[2,64,1536]{2,1,0:T(8,128)(2,1)} %bitcast.3, ...), custom_call_target="tpu_custom_call" | custom-call | tf_op jit(solution)/shard_map/pallas_call | solution.py:1074
  258.1 3.1 %shard_map.282 = (bf16[1,2,1,64,1536]{4,3,2,1,0:T(8,128)(2,1)}, bf16[1,2,1,64,1536]{4,3,2,1,0:T(8,128)(2,1)}, f32[1,24]{1,0:T(1,128)}, f32[1,24]{1,0:T(1,128)}, ...) custom-call(bf16[2,64,1536]{2,1,0:T(8,128)(2,1)} %get-tuple-element., ...), custom_call_target="tpu_custom_call" | custom-call | tf_op jit(solution)/shard_map/pallas_call | solution.py:1112
